TPU v7x, 32 devices: a whole 2x2x4 slice. The times are simulated.
32 devices in a mesh: row: 4 (over z), col: 8 (over y, x, core).
Axes of the slice: x: 2, y: 2, z: 4, core: 2. Of those that a mesh axis runs over, the one named last changes fastest.
Arguments:
- layer_input: bfloat16 [512, 8192], P('col', 'row'), may hold values from -6 to 6
- out_grad: bfloat16 [512, 8192], P('col', 'row'), may hold values from -6 to 6
- gate_saved: bfloat16 [512, 14336], P('row', 'col'), may hold values from -8 to 8
- up_saved: bfloat16 [512, 14336], P('row', 'col'), may hold values from -6 to 6
- gate_weight: bfloat16 [8192, 14336], P('row', 'col'), may hold values from -0.0625 to 0.0625
- up_weight: bfloat16 [8192, 14336], P('row', 'col'), may hold values from -0.0625 to 0.0625
- down_weight: bfloat16 [14336, 8192], P('col', 'row'), may hold values from -0.046875 to 0.046875
Outputs:
- input_grad: bfloat16 [512, 8192], P('col', 'row')
- gate_weight_grad: float32 [8192, 14336], P('row', 'col')
- up_weight_grad: float32 [8192, 14336], P('row', 'col')
- down_weight_grad: float32 [14336, 8192], P('col', 'row')
All inputs are finite; a program needn't handle non-finite values.
Results may differ from a plain program's by a relative error of at most 0.02.
Values may be sent and summed in bfloat16 or wider, within the bound.
No kernel may reach another device: no remote copies, remote signals or barrier semaphores. Data moves between devices by JAX's collectives and lax.ppermute only.
A program may use at most 128 MiB of HBM per device.

v0:
```python
import jax
import jax.numpy as jnp
from jax import lax
from jax.experimental import pallas as pl
from jax.experimental.pallas import tpu as pltpu
from jax.sharding import PartitionSpec as P

CHUNKS = 2
VMEM = 60 * 1024 * 1024


def tile_of(size, limit):
    return max(t for t in range(128, limit + 1, 128) if size % t == 0)


def params():
    return pltpu.CompilerParams(vmem_limit_bytes=VMEM)


def cost(flops, moved):
    return pl.CostEstimate(flops=flops, bytes_accessed=moved, transcendentals=0)


def dot(left, right, dims):
    return lax.dot_general(left, right, (dims, ((), ())), preferred_element_type=jnp.float32)


def halves_of(size):
    cut = max(size // 2 // 256 * 256, 128)
    return slice(0, size - cut), slice(size - cut, size)


def sigmoid(gate):
    return 1.0 / (1.0 + jnp.exp(-gate))


def hidden_grad_terms(q, pieces, others, axis, down):
    half = len(pieces)
    _, rows, depth = pieces[0].shape
    wide = down.shape[0]
    tokens = 2 * half * rows
    tile = tile_of(wide, 896)

    def body(*refs):
        down_ref, out_ref, grad_ref = refs[2 * half :]

        @pl.when(pl.program_id(0) == 0)
        def _():
            here = lax.axis_index(axis)
            for k in range(half):
                grad_ref[here ^ (2 * k)] = refs[k][...]
                grad_ref[here ^ (2 * k + 1)] = refs[half + k][...]

        left = grad_ref[...].reshape(tokens, depth)
        out_ref[...] = dot(left, down_ref[...], ((1,), (1,))).astype(jnp.bfloat16)

    return pl.pallas_call(
        body,
        grid=(wide // tile,),
        in_specs=[pl.BlockSpec((None, rows, depth), lambda i: (q, 0, 0))] * (2 * half)
        + [pl.BlockSpec((tile, depth), lambda i: (i, 0))],
        out_specs=pl.BlockSpec((tokens, tile), lambda i: (0, i)),
        out_shape=jax.ShapeDtypeStruct((tokens, wide), jnp.bfloat16),
        scratch_shapes=[pltpu.VMEM((2 * half, rows, depth), jnp.bfloat16)],
        compiler_params=params(),
        cost_estimate=cost(2 * tokens * depth * wide, 2 * (down.size + tokens * depth)),
        name="hidden_grad_terms",
    )(*pieces, *others, down)


def down_weight_grads(saved, places, grad, axis, scale):
    blocks, _, _, wide = saved[0][0].shape
    cols, chunks, rows, depth = grad.shape
    tokens = chunks * cols * rows
    tile = tile_of(wide, 256)
    flat = [x for shard in saved for x in shard]
    n = len(flat)

    def body(*refs):
        saved_refs = list(refs[:n])
        grad_ref, out_ref, by_gate_ref, by_up_ref, hidden_ref = refs[n:]
        for k, (shard, there) in enumerate(places(lax.axis_index(axis))):
            pair = [saved_refs.pop(0) for _ in saved[k]]
            gate_ref, up_ref = pair if len(pair) == 2 else (pair[0].at[0], pair[0].at[1])

            @pl.when(there)
            def _():
                gate_val = gate_ref[...].astype(jnp.float32)
                up_val = up_ref[...].astype(jnp.float32)
                sigma = sigmoid(gate_val)
                silu = gate_val * sigma
                slope = sigma * (1.0 + gate_val * (1.0 - sigma))
                to = pl.ds(shard * blocks, blocks)
                hidden_ref[to] = (silu * up_val).astype(jnp.bfloat16)
                by_gate_ref[to] = (up_val * slope).astype(jnp.bfloat16)
                by_up_ref[to] = silu.astype(jnp.bfloat16)

        left = hidden_ref[...].reshape(tokens, tile)
        right = grad_ref[...].reshape(tokens, depth)
        out_ref[...] = scale * dot(left, right, ((0,), (0,)))

    one = pl.BlockSpec((blocks, chunks, rows, tile), lambda i: (0, 0, 0, i))
    two = pl.BlockSpec((2, blocks, chunks, rows, tile), lambda i: (0, 0, 0, 0, i))
    factor = pl.BlockSpec((cols, chunks, rows, tile), lambda i: (0, 0, 0, i))
    factors = jax.ShapeDtypeStruct((cols, chunks, rows, wide), jnp.bfloat16)
    return pl.pallas_call(
        body,
        grid=(wide // tile,),
        in_specs=[one if x.ndim == 4 else two for x in flat]
        + [pl.BlockSpec((cols, chunks, rows, depth), lambda i: (0, 0, 0, 0))],
        out_specs=[pl.BlockSpec((tile, depth), lambda i: (i, 0)), factor, factor],
        out_shape=[jax.ShapeDtypeStruct((wide, depth), jnp.float32), factors, factors],
        scratch_shapes=[pltpu.VMEM((cols, chunks, rows, tile), jnp.bfloat16)],
        compiler_params=params(),
        cost_estimate=cost(2 * tokens * wide * depth, 4 * wide * depth),
        name="down_weight_grads",
    )(*flat, grad)


def input_grad_terms(q, sums, by_gate, by_up, gate_weight, up_weight, axes, made):
    cols, chunks, rows, wide = by_gate.shape
    depth = gate_weight.shape[0]
    tokens = cols * rows
    levels = len(sums)
    tile = tile_of(depth, 512)

    def body(*refs):
        sums_refs, refs = refs[:levels], refs[levels:]
        by_gate_ref, by_up_ref, gate_w_ref, up_w_ref = refs[:4]
        gate_out, up_out, keep_ref, send_ref = refs[-4:]

        @pl.when(pl.program_id(0) == 0)
        def _():
            here = lax.axis_index(axes[0])
            hidden_grad = sums_refs[0][...].astype(jnp.float32)
            for level in range(1, levels):
                at_level = (here == levels - 1 - level) | (here == levels + level)
                other = sums_refs[level][...].astype(jnp.float32)
                hidden_grad = jnp.where(at_level, other, hidden_grad)
            for by_ref, out in ((by_gate_ref, gate_out), (by_up_ref, up_out)):
                by = by_ref[...].reshape(tokens, wide).astype(jnp.float32)
                out[...] = (hidden_grad * by).astype(jnp.bfloat16).reshape(cols, rows, wide)

        odd = lax.axis_index(axes[1]) % 2 == 1
        gate_grad = gate_out[...].reshape(tokens, wide)
        up_grad = up_out[...].reshape(tokens, wide)
        for part in halves_of(tile):
            res = dot(gate_grad, gate_w_ref[part], ((1,), (1,)))
            res += dot(up_grad, up_w_ref[part], ((1,), (1,)))
            res = res.astype(jnp.bfloat16).reshape(cols // 2, 2, rows, part.stop - part.start)
            keep_ref[:, :, part] = jnp.where(odd, res[:, 1], res[:, 0])
            send_ref[:, :, part] = jnp.where(odd, res[:, 0], res[:, 1])

    into = pl.BlockSpec((cols, None, rows, wide), lambda i: (0, q, 0, 0))
    weight = pl.BlockSpec((tile, wide), lambda i: (i, 0))
    half = pl.BlockSpec((cols // 2, rows, tile), lambda i: (0, 0, i))
    halves = jax.ShapeDtypeStruct((cols // 2, rows, depth), jnp.bfloat16)
    whole = jax.ShapeDtypeStruct((cols, chunks, rows, wide), jnp.bfloat16)
    return pl.pallas_call(
        body,
        grid=(depth // tile,),
        in_specs=[pl.BlockSpec((tokens, wide), lambda i: (0, 0))] * levels
        + [into, into, weight, weight]
        + [pl.BlockSpec(memory_space=pl.ANY)] * len(made),
        out_specs=[into, into, half, half],
        out_shape=[whole, whole, halves, halves],
        input_output_aliases={levels + 4 + j: j for j in range(len(made))},
        compiler_params=params(),
        cost_estimate=cost(4 * tokens * wide * depth, 4 * wide * depth),
        name="input_grad_terms",
    )(*sums, by_gate, by_up, gate_weight, up_weight, *made)


def projection_grads(inputs, gate_grad, up_grad, scale):
    depth, tokens = inputs.shape
    wide = gate_grad.shape[1]
    tile = tile_of(depth, 256)

    def body(inputs_ref, gate_ref, up_ref, gate_out, up_out):
        left = inputs_ref[...]
        gate_out[...] = scale * dot(left, gate_ref[...], ((1,), (0,)))
        up_out[...] = scale * dot(left, up_ref[...], ((1,), (0,)))

    once = pl.BlockSpec((tokens, wide), lambda i: (0, 0))
    out = pl.BlockSpec((tile, wide), lambda i: (i, 0))
    return pl.pallas_call(
        body,
        grid=(depth // tile,),
        in_specs=[pl.BlockSpec((tile, tokens), lambda i: (i, 0)), once, once],
        out_specs=[out, out],
        out_shape=[jax.ShapeDtypeStruct((depth, wide), jnp.float32)] * 2,
        compiler_params=params(),
        cost_estimate=cost(4 * tokens * wide * depth, 8 * wide * depth),
        name="projection_grads",
    )(inputs, gate_grad, up_grad)


def gather_places(size):
    def places(here):
        if size != 4:
            return [(here ^ k, True) for k in range(size)]
        outer = (here == 0) | (here == 3)
        inner = jnp.logical_not(outer)
        return [
            (here, True),
            (here ^ 1, True),
            (here ^ 3, inner),
            (here ^ 2, inner),
            (here ^ 2, outer),
            (here ^ 3, outer),
        ]

    return places


def gather_near(shard, axis, size):
    if size == 4:
        swaps = [[(i, i ^ 1) for i in range(size)], [(1, 2), (2, 1)]]
    else:
        swaps = [[(i, i ^ k) for i in range(size)] for k in range(1, size)]
    return [shard] + [lax.ppermute(shard, axis, pairs) for pairs in swaps]


def trade(term, shards, axis):
    here = lax.axis_index(axis)
    outer = (here == 0) | (here == 3)
    given = jnp.where(outer, term, shards.reshape(term.shape))
    return lax.ppermute(given, axis, [(i, i ^ 1) for i in range(4)])


def both(left, right):
    return (left.astype(jnp.float32) + right.astype(jnp.float32)).astype(jnp.bfloat16)


def sum_in(term, axis, size):
    total = term
    for k in range(size // 2 - 1):
        got = lax.ppermute(total, axis, [(k, k + 1), (size - 1 - k, size - 2 - k)])
        total = both(term, got)
    return total


def sum_swap(total, axis, size):
    half = size // 2
    return both(total, lax.ppermute(total, axis, [(half - 1, half), (half, half - 1)]))


def sum_out(total, axis, size):
    found = [total]
    for k in reversed(range(size // 2 - 1)):
        found.append(lax.ppermute(found[-1], axis, [(k + 1, k), (size - 2 - k, size - 1 - k)]))
    return found


def scatter_halves(keep, send, axis, size):
    return both(keep, lax.ppermute(send, axis, [(i, i ^ 1) for i in range(size)]))


def scatter_sum(halves, axis, size):
    here = lax.axis_index(axis)

    def block(k):
        at = (here // 2) ^ k
        return jnp.concatenate(
            [lax.dynamic_index_in_dim(x, at, 0, keepdims=False) for x in halves], axis=0
        )

    total = block(0).astype(jnp.float32)
    for k in range(1, size // 2):
        got = lax.ppermute(block(k), axis, [(i, i ^ (2 * k)) for i in range(size)])
        total += got.astype(jnp.float32)
    return total.astype(jnp.bfloat16)


def hold(*values):
    return lax.optimization_barrier(values)


def solution(mesh):
    n_row, n_col = mesh.shape["row"], mesh.shape["col"]

    def shards(layer_input, out_grad, gate_saved, up_saved, gate_weight, up_weight, down_weight):
        block, depth = layer_input.shape
        row_tokens, wide = gate_saved.shape
        tokens = block * n_col
        rows = block // CHUNKS
        scale = float(tokens) ** (-0.5)
        weights = (gate_weight, up_weight, ("row", "col"))

        view = (row_tokens // block, CHUNKS, rows, wide)
        gates = gather_near(gate_saved.reshape(view), "row", n_row)
        up_saved = up_saved.reshape(view)
        own = out_grad.reshape(CHUNKS, rows, depth)
        pieces = [own] + [
            lax.ppermute(own, "col", [(i, i ^ (2 * k)) for i in range(n_col)])
            for k in range(1, n_col // 2)
        ]
        pieces, gates, up_saved, out_grad, layer_input = hold(
            pieces, gates, up_saved, out_grad, layer_input
        )
        ups = gather_near(up_saved, "row", n_row)
        others = [lax.ppermute(x, "col", [(i, i ^ 1) for i in range(n_col)]) for x in pieces]
        grad = lax.all_gather(out_grad, "col", axis=0, tiled=True)
        inputs = lax.all_gather(layer_input, "col", axis=0, tiled=True)
        first = hidden_grad_terms(0, pieces, others, "col", down_weight)
        first, gates, ups, pieces, others = hold(first, gates, ups, pieces, others)

        line = n_row == 4 and 2 * row_tokens * CHUNKS == tokens
        saved = [list(pair) for pair in zip(gates, ups)]
        if line:
            got = trade(first, jnp.stack([gates[2], ups[2]]), "row")
            passed = lax.ppermute(jnp.stack([gates[1], ups[1]]), "row", [(1, 2), (2, 1)])
            first = both(first, got)
            saved += [[passed], [got.reshape(passed.shape)]]
        else:
            first = sum_in(first, "row", n_row)
        second = hidden_grad_terms(1, pieces, others, "col", down_weight)
        first, second, saved = hold(first, second, saved)

        if line:
            got = trade(second, saved[3][0], "row")
            second = both(second, got)
            saved += [[got.reshape(saved[3][0].shape)]]
        else:
            second = sum_in(second, "row", n_row)
        first = sum_swap(first, "row", n_row)
        first, second, grad, saved = hold(first, second, grad, saved)

        first = sum_out(first, "row", n_row)
        second = sum_swap(second, "row", n_row)
        grad = grad.reshape(n_col, CHUNKS, rows, depth)
        down_weight_grad, *factors = down_weight_grads(
            saved, gather_places(n_row), grad, "row", scale
        )
        first, second, down_weight_grad, factors, inputs = hold(
            first, second, down_weight_grad, factors, inputs
        )

        second = sum_out(second, "row", n_row)
        *made, keep, send = input_grad_terms(0, first, *factors, *weights, ())
        inputs = inputs.T
        second, made, keep, send, inputs = hold(second, made, keep, send, inputs)

        early = scatter_halves(keep, send, "col", n_col)
        *made, keep, send = input_grad_terms(1, second, *factors, *weights, made)
        early, made, keep, send = hold(early, made, keep, send)
        late = scatter_halves(keep, send, "col", n_col)
        late, made = hold(late, made)
        input_grad = scatter_sum([early, late], "col", n_col)
        made = [x.reshape(tokens, wide) for x in made]
        gate_weight_grad, up_weight_grad = projection_grads(inputs, *made, scale)
        return input_grad, gate_weight_grad, up_weight_grad, down_weight_grad

    by_token, by_unit = P("col", "row"), P("row", "col")
    return jax.shard_map(
        shards,
        mesh=mesh,
        in_specs=(by_token, by_token, by_unit, by_unit, by_unit, by_unit, by_token),
        out_specs=(by_token, by_unit, by_unit, by_token),
        check_vma=False,
    )
```

profile of v0, /device:TPU:0, one launch (start us, length us, event | category | flops | bytes accessed | tf_op | source)
XLA Modules:
  0.0 178.1 jit_solution(8305022030366901387)
XLA Ops:
  7.9 5.9 %collective-permute-start.3 = (bf16[2,2,32,1792]{3,2,1,0:T(8,128)(2,1)}, bf16[2,2,32,1792]{3,2,1,0:T(8,128)(2,1)S(1)}, u32[]{:S(2)}, u32[]{:S(2)}) collective-permute-start(bf16[2,2,32,1792]{3,2,1,0:T(8,128)(2,1)} %bitcast.50), channel_id=1, source_target_pairs={{0,8},{8,0},{16,24},{24,16},{1,9},{9,1},{17,25},{25,17},{2,10},{10... | collective-permute-start | bytes 1376264 | tf_op jit(solution)/shard_map/ppermute | solution.py:221
  13.8 2.4 %collective-permute-start.2 = (bf16[2,32,2048]{2,1,0:T(8,128)(2,1)}, bf16[2,32,2048]{2,1,0:T(8,128)(2,1)S(1)}, u32[]{:S(2)}, u32[]{:S(2)}) collective-permute-start(bf16[2,32,2048]{2,1,0:T(8,128)(2,1)} %bitcast.33), channel_id=1, source_target_pairs={{0,6},{1,7},{2,4},{3,5},{4,2},{5,3},{6,0},{7,1},{8,14},{9,15},{10,... | collective-permute-start | bytes 786440 | tf_op jit(solution)/shard_map/ppermute | solution.py:295
  17.3 6.9 %collective-permute-done.2.refs_3_ = bf16[2,32,2048]{2,1,0:T(8,128)(2,1)S(1)} collective-permute-done((bf16[2,32,2048]{2,1,0:T(8,128)(2,1)}, bf16[2,32,2048]{2,1,0:T(8,128)(2,1)S(1)}, u32[]{:S(2)}, u32[]{:S(2)}) %collective-permute-start.2) | collective-permute-done | bytes 262176 | tf_op jit(solution)/shard_map/ppermute | solution.py:295
  24.2 3.8 %collective-permute-done.1.refs_2_ = bf16[2,32,2048]{2,1,0:T(8,128)(2,1)S(1)} collective-permute-done((bf16[2,32,2048]{2,1,0:T(8,128)(2,1)}, bf16[2,32,2048]{2,1,0:T(8,128)(2,1)S(1)}, u32[]{:S(2)}, u32[]{:S(2)}) %collective-permute-start.1) | collective-permute-done | bytes 262176 | tf_op jit(solution)/shard_map/ppermute | solution.py:295
  29.0 1.4 collective-permute-start.10
  30.4 1.4 collective-permute-start.9
  32.3 0.9 collective-permute-done.6.refs_5_
  35.1 5.7 %hidden_grad_terms.2 = bf16[256,1792]{1,0:T(8,128)(2,1)} custom-call(bf16[2,32,2048]{2,1,0:T(8,128)(2,1)} %bitcast.37, bf16[2,32,2048]{2,1,0:T(8,128)(2,1)} %copy-done.6, bf16[2,32,2048]{2,1,0:T(8,128)(2,1)} %copy-done.5, bf16[2,32,2048]{2,1,0:T(8,128)(2,1)} %copy-done.4, bf16[2,32,2048]{2,1,0:T(8,128)(2,1)} %copy-done.7, bf16[2,32,2048]{2,1,0:T(8,128)(2,1)} %copy-done.8, ...), custom_call_target="tpu_custom_call" | custom-call | flops 1879048192 | bytes 8388608 | tf_op jit(solution)/shard_map/hidden_grad_terms/pallas_call | solution.py:57
  40.8 2.8 %collective-permute-done.9.refs_3_ = bf16[2,2,32,1792]{3,2,1,0:T(8,128)(2,1)} collective-permute-done((bf16[2,2,32,1792]{3,2,1,0:T(8,128)(2,1)}, bf16[2,2,32,1792]{3,2,1,0:T(8,128)(2,1)}, u32[]{:S(2)}, u32[]{:S(2)}) %collective-permute-start.9) | collective-permute-done | bytes 458784 | tf_op jit(solution)/shard_map/ppermute | solution.py:221
  43.6 1.1 pad_maximum_fusion
  44.8 1.1 bitcast_select_fusion.1
  45.8 1.1 collective-permute-start.11
  46.9 1.1 pad_maximum_fusion.1
  48.8 5.8 %hidden_grad_terms.3 = bf16[256,1792]{1,0:T(8,128)(2,1)} custom-call(bf16[2,32,2048]{2,1,0:T(8,128)(2,1)} %bitcast.38, bf16[2,32,2048]{2,1,0:T(8,128)(2,1)} %copy-done.6, bf16[2,32,2048]{2,1,0:T(8,128)(2,1)} %copy-done.5, bf16[2,32,2048]{2,1,0:T(8,128)(2,1)} %copy-done.4, bf16[2,32,2048]{2,1,0:T(8,128)(2,1)} %copy-done.7, bf16[2,32,2048]{2,1,0:T(8,128)(2,1)} %copy-done.8, ...), custom_call_target="tpu_custom_call" | custom-call | flops 1879048192 | bytes 8388608 | tf_op jit(solution)/shard_map/hidden_grad_terms/pallas_call | solution.py:57
  54.6 13.5 %collective-permute-done.11 = bf16[256,1792]{1,0:T(8,128)(2,1)} collective-permute-done((bf16[256,1792]{1,0:T(8,128)(2,1)}, bf16[256,1792]{1,0:T(8,128)(2,1)}, u32[]{:S(2)}, u32[]{:S(2)}) %collective-permute-start.11) | collective-permute-done | bytes 917536 | tf_op jit(solution)/shard_map/ppermute | solution.py:228
  68.1 1.4 add_convert_fusion.3
  69.7 3.1 %collective-permute-start.14 = (bf16[256,1792]{1,0:T(8,128)(2,1)S(1)}, bf16[256,1792]{1,0:T(8,128)(2,1)S(1)}, u32[]{:S(2)}, u32[]{:S(2)}) collective-permute-start(bf16[256,1792]{1,0:T(8,128)(2,1)S(1)} %bitcast_select_fusion), channel_id=1, source_target_pairs={{0,8},{8,0},{16,24},{24,16},{1,9},{9,1},{17,25},{25,17},{2,10},{10... | collective-permute-start | bytes 2752520 | tf_op jit(solution)/shard_map/ppermute | solution.py:228
  73.5 18.4 %collective-permute-done.14 = bf16[256,1792]{1,0:T(8,128)(2,1)S(1)} collective-permute-done((bf16[256,1792]{1,0:T(8,128)(2,1)S(1)}, bf16[256,1792]{1,0:T(8,128)(2,1)S(1)}, u32[]{:S(2)}, u32[]{:S(2)}) %collective-permute-start.14) | collective-permute-done | bytes 917536 | tf_op jit(solution)/shard_map/ppermute | solution.py:228
  93.2 1.6 collective-permute-start.16
  94.8 1.3 collective-permute-start.15
  96.1 13.6 %down_weight_grads.1 = (f32[1792,2048]{1,0:T(8,128)}, bf16[8,2,32,1792]{3,2,1,0:T(8,128)(2,1)}, bf16[8,2,32,1792]{3,2,1,0:T(8,128)(2,1)}) custom-call(bf16[2,2,32,1792]{3,2,1,0:T(8,128)(2,1)} %bitcast.51, bf16[2,2,32,1792]{3,2,1,0:T(8,128)(2,1)} %bitcast.48, bf16[2,2,32,1792]{3,2,1,0:T(8,128)(2,1)} %copy-done.17, ...), custom_call_target="tpu_custom_call" | custom-call | flops 3758096384 | bytes 14680064 | tf_op jit(solution)/shard_map/down_weight_grads/pallas_call | solution.py:106
  109.7 1.4 add_convert_fusion.refs_0_
  111.2 6.9 %collective-permute-done.15.refs_1_ = bf16[256,1792]{1,0:T(8,128)(2,1)} collective-permute-done((bf16[256,1792]{1,0:T(8,128)(2,1)S(1)}, bf16[256,1792]{1,0:T(8,128)(2,1)}, u32[]{:S(2)}, u32[]{:S(2)}) %collective-permute-start.15) | collective-permute-done | bytes 917536 | tf_op jit(solution)/shard_map/ppermute | solution.py:251
  118.1 1.3 collective-permute-start.17
  119.4 3.9 %copy.14 = bf16[512,2048]{0,1:T(8,128)(2,1)} copy(bf16[512,2048]{1,0:T(8,128)(2,1)} %all-gather.5.cloned.1.call-done) | data formatting | bytes 4194304 | tf_op jit(solution)/shard_map/optimization_barrier | solution.py:276
  123.3 10.8 %input_grad_terms.2 = (bf16[8,2,32,1792]{3,2,1,0:T(8,128)(2,1)}, bf16[8,2,32,1792]{3,2,1,0:T(8,128)(2,1)}, bf16[4,32,2048]{2,1,0:T(8,128)(2,1)}, bf16[4,32,2048]{2,1,0:T(8,128)(2,1)}) custom-call(bf16[256,1792]{1,0:T(8,128)(2,1)} %copy-done.2, bf16[256,1792]{1,0:T(8,128)(2,1)} %collective-permute-done.15.refs_1_, ...), custom_call_target="tpu_custom_call" | custom-call | flops 3758096384 | bytes 14680064 | tf_op jit(solution)/shard_map/input_grad_terms/pallas_call | solution.py:159
  134.1 4.9 %collective-permute-done.17.refs_1_ = bf16[256,1792]{1,0:T(8,128)(2,1)S(1)} collective-permute-done((bf16[256,1792]{1,0:T(8,128)(2,1)S(1)}, bf16[256,1792]{1,0:T(8,128)(2,1)S(1)}, u32[]{:S(2)}, u32[]{:S(2)}) %collective-permute-start.17) | collective-permute-done | bytes 917536 | tf_op jit(solution)/shard_map/ppermute | solution.py:251
  139.9 10.8 %input_grad_terms.3 = (bf16[8,2,32,1792]{3,2,1,0:T(8,128)(2,1)}, bf16[8,2,32,1792]{3,2,1,0:T(8,128)(2,1)}, bf16[4,32,2048]{2,1,0:T(8,128)(2,1)}, bf16[4,32,2048]{2,1,0:T(8,128)(2,1)}) custom-call(bf16[256,1792]{1,0:T(8,128)(2,1)} %copy-done.3, bf16[256,1792]{1,0:T(8,128)(2,1)} %copy-done.13, ...), custom_call_target="tpu_custom_call", output_to_operand_aliasing={{0}: (6, {}), {1}: (7, {})} | custom-call | flops 3758096384 | bytes 14680064 | tf_op jit(solution)/shard_map/input_grad_terms/pallas_call | solution.py:159
  151.1 2.0 %collective-permute-done.19 = bf16[4,32,2048]{2,1,0:T(8,128)(2,1)S(1)} collective-permute-done((bf16[4,32,2048]{2,1,0:T(8,128)(2,1)}, bf16[4,32,2048]{2,1,0:T(8,128)(2,1)S(1)}, u32[]{:S(2)}, u32[]{:S(2)}) %collective-permute-start.19) | collective-permute-done | bytes 524320 | tf_op jit(solution)/shard_map/ppermute | solution.py:256
  153.3 1.5 collective-permute-start.20
  155.6 1.4 collective-permute-start.22
  157.0 13.4 %projection_grads.1 = (f32[2048,1792]{1,0:T(8,128)}, f32[2048,1792]{1,0:T(8,128)}) custom-call(bf16[2048,512]{1,0:T(8,128)(2,1)} %bitcast.39, bf16[512,1792]{1,0:T(8,128)(2,1)} %bitcast.40, bf16[512,1792]{1,0:T(8,128)(2,1)} %bitcast.41), custom_call_target="tpu_custom_call" | custom-call | flops 7516192768 | bytes 29360128 | tf_op jit(solution)/shard_map/projection_grads/pallas_call | solution.py:186
  (81 shorter events, 11.0 us)
Async XLA Ops:
  7.2 86.0 %all-gather.3.cloned.1.call-start = ((), (), s32[]{:S(2)}) async-start(), calls=%async_computation | async-start | bytes 2359296 | tf_op jit(solution)/shard_map/all_gather | solution.py:303
  7.2 20.9 %collective-permute-start.4 = (bf16[2,2,32,1792]{3,2,1,0:T(8,128)(2,1)}, bf16[2,2,32,1792]{3,2,1,0:T(8,128)(2,1)S(1)}, u32[]{:S(2)}, u32[]{:S(2)}) collective-permute-start(bf16[2,2,32,1792]{3,2,1,0:T(8,128)(2,1)} %bitcast.49), channel_id=1, source_target_pairs={{8,16},{16,8},{9,17},{17,9},{10,18},{18,10},{11,19},{19,11},{12,20... | collective-permute-start | bytes 1376264 | tf_op jit(solution)/shard_map/ppermute | solution.py:221
  7.9 20.2 %collective-permute-start.3 = (bf16[2,2,32,1792]{3,2,1,0:T(8,128)(2,1)}, bf16[2,2,32,1792]{3,2,1,0:T(8,128)(2,1)S(1)}, u32[]{:S(2)}, u32[]{:S(2)}) collective-permute-start(bf16[2,2,32,1792]{3,2,1,0:T(8,128)(2,1)} %bitcast.50), channel_id=1, source_target_pairs={{0,8},{8,0},{16,24},{24,16},{1,9},{9,1},{17,25},{25,17},{2,10},{10... | collective-permute-start | bytes 1376264 | tf_op jit(solution)/shard_map/ppermute | solution.py:221
  13.8 10.4 %collective-permute-start.2 = (bf16[2,32,2048]{2,1,0:T(8,128)(2,1)}, bf16[2,32,2048]{2,1,0:T(8,128)(2,1)S(1)}, u32[]{:S(2)}, u32[]{:S(2)}) collective-permute-start(bf16[2,32,2048]{2,1,0:T(8,128)(2,1)} %bitcast.33), channel_id=1, source_target_pairs={{0,6},{1,7},{2,4},{3,5},{4,2},{5,3},{6,0},{7,1},{8,14},{9,15},{10,... | collective-permute-start | bytes 786440 | tf_op jit(solution)/shard_map/ppermute | solution.py:295
  16.2 11.8 %collective-permute-start.1 = (bf16[2,32,2048]{2,1,0:T(8,128)(2,1)}, bf16[2,32,2048]{2,1,0:T(8,128)(2,1)S(1)}, u32[]{:S(2)}, u32[]{:S(2)}) collective-permute-start(bf16[2,32,2048]{2,1,0:T(8,128)(2,1)} %bitcast.34), channel_id=1, source_target_pairs={{0,4},{1,5},{2,6},{3,7},{4,0},{5,1},{6,2},{7,3},{8,12},{9,13},{10,... | collective-permute-start | bytes 786440 | tf_op jit(solution)/shard_map/ppermute | solution.py:295
  16.7 11.4 %collective-permute-start = (bf16[2,32,2048]{2,1,0:T(8,128)(2,1)}, bf16[2,32,2048]{2,1,0:T(8,128)(2,1)S(1)}, u32[]{:S(2)}, u32[]{:S(2)}) collective-permute-start(bf16[2,32,2048]{2,1,0:T(8,128)(2,1)} %bitcast.35), channel_id=1, source_target_pairs={{0,2},{1,3},{2,0},{3,1},{4,6},{5,7},{6,4},{7,5},{8,10},{9,11},{10,... | collective-permute-start | bytes 786440 | tf_op jit(solution)/shard_map/ppermute | solution.py:295
  24.2 9.8 %copy-start.4 = (bf16[2,32,2048]{2,1,0:T(8,128)(2,1)}, bf16[2,32,2048]{2,1,0:T(8,128)(2,1)S(1)}, u32[]{:S(2)}) copy-start(bf16[2,32,2048]{2,1,0:T(8,128)(2,1)S(1)} %collective-permute-done.2.refs_3_) | copy-start | bytes 786436
  28.1 16.6 %copy-start.16 = (bf16[2,2,32,1792]{3,2,1,0:T(8,128)(2,1)}, bf16[2,2,32,1792]{3,2,1,0:T(8,128)(2,1)S(1)}, u32[]{:S(2)}) copy-start(bf16[2,2,32,1792]{3,2,1,0:T(8,128)(2,1)S(1)} %collective-permute-done.4.refs_4_) | copy-start | bytes 1376260
  28.9 82.2 %all-gather.5.cloned.1.call-start = ((), (), s32[]{:S(2)}) async-start(), calls=%async_computation.1 | async-start | bytes 2359296 | tf_op jit(solution)/shard_map/all_gather | solution.py:304
  29.0 3.3 %collective-permute-start.5 = (bf16[2,32,2048]{2,1,0:T(8,128)(2,1)}, bf16[2,32,2048]{2,1,0:T(8,128)(2,1)S(1)}, u32[]{:S(2)}, u32[]{:S(2)}) collective-permute-start(bf16[2,32,2048]{2,1,0:T(8,128)(2,1)} %bitcast.36), channel_id=1, source_target_pairs={{0,1},{1,0},{2,3},{3,2},{4,5},{5,4},{6,7},{7,6},{8,9},{9,8},{10,11... | collective-permute-start | bytes 786440 | tf_op jit(solution)/shard_map/ppermute | solution.py:302
  29.0 11.8 %collective-permute-start.10 = (bf16[2,2,32,1792]{3,2,1,0:T(8,128)(2,1)}, bf16[2,2,32,1792]{3,2,1,0:T(8,128)(2,1)}, u32[]{:S(2)}, u32[]{:S(2)}) collective-permute-start(bf16[2,2,32,1792]{3,2,1,0:T(8,128)(2,1)} %bitcast.46), channel_id=1, source_target_pairs={{8,16},{16,8},{9,17},{17,9},{10,18},{18,10},{11,19},{19,11},{12,20... | collective-permute-start | bytes 1376264 | tf_op jit(solution)/shard_map/ppermute | solution.py:221
  30.4 13.2 %collective-permute-start.9 = (bf16[2,2,32,1792]{3,2,1,0:T(8,128)(2,1)}, bf16[2,2,32,1792]{3,2,1,0:T(8,128)(2,1)}, u32[]{:S(2)}, u32[]{:S(2)}) collective-permute-start(bf16[2,2,32,1792]{3,2,1,0:T(8,128)(2,1)} %bitcast.47), channel_id=1, source_target_pairs={{0,8},{8,0},{16,24},{24,16},{1,9},{9,1},{17,25},{25,17},{2,10},{10... | collective-permute-start | bytes 1376264 | tf_op jit(solution)/shard_map/ppermute | solution.py:221
  31.7 1.5 collective-permute-start.6
  31.7 1.9 %collective-permute-start.7 = (bf16[2,32,2048]{2,1,0:T(8,128)(2,1)S(1)}, bf16[2,32,2048]{2,1,0:T(8,128)(2,1)S(1)}, u32[]{:S(2)}, u32[]{:S(2)}) collective-permute-start(bf16[2,32,2048]{2,1,0:T(8,128)(2,1)S(1)} %collective-permute-done.1.refs_2_), channel_id=1, source_target_pairs={{0,1},{1,0},{2,3},{3,2},{4,5},{5,4},{6,7},{7,6},{8,9},{9,8},{10,11... | collective-permute-start | bytes 786440 | tf_op jit(solution)/shard_map/ppermute | solution.py:302
  32.3 1.8 collective-permute-start.8
  45.8 22.3 %collective-permute-start.11 = (bf16[256,1792]{1,0:T(8,128)(2,1)}, bf16[256,1792]{1,0:T(8,128)(2,1)}, u32[]{:S(2)}, u32[]{:S(2)}) collective-permute-start(bf16[256,1792]{1,0:T(8,128)(2,1)} %bitcast_select_fusion.1), channel_id=1, source_target_pairs={{0,8},{8,0},{16,24},{24,16},{1,9},{9,1},{17,25},{25,17},{2,10},{10... | collective-permute-start | bytes 2752520 | tf_op jit(solution)/shard_map/ppermute | solution.py:228
  48.0 21.5 %collective-permute-start.12 = (bf16[2,2,2,32,1792]{4,3,2,1,0:T(8,128)(2,1)S(1)}, bf16[2,2,2,32,1792]{4,3,2,1,0:T(8,128)(2,1)S(1)}, u32[]{:S(2)}, u32[]{:S(2)}) collective-permute-start(bf16[2,2,2,32,1792]{4,3,2,1,0:T(8,128)(2,1)S(1)} %pad_maximum_fusion.1), channel_id=1, source_target_pairs={{8,16},{16,8},{9,17},{17,9},{10,18},{18,10},{11,19},{19,11},{12,20... | collective-permute-start | bytes 2752520 | tf_op jit(solution)/shard_map/ppermute | solution.py:312
  54.6 15.0 %copy-start.1 = (bf16[256,1792]{1,0:T(8,128)(2,1)S(1)}, bf16[256,1792]{1,0:T(8,128)(2,1)}, u32[]{:S(2)}) copy-start(bf16[256,1792]{1,0:T(8,128)(2,1)} %hidden_grad_terms.3) | copy-start | bytes 2752516
  69.5 22.6 %copy-start.11 = (bf16[2,2,2,32,1792]{4,3,2,1,0:T(8,128)(2,1)}, bf16[2,2,2,32,1792]{4,3,2,1,0:T(8,128)(2,1)S(1)}, u32[]{:S(2)}) copy-start(bf16[2,2,2,32,1792]{4,3,2,1,0:T(8,128)(2,1)S(1)} %collective-permute-done.12.refs_6_) | copy-start | bytes 2752516
  69.7 22.2 %collective-permute-start.14 = (bf16[256,1792]{1,0:T(8,128)(2,1)S(1)}, bf16[256,1792]{1,0:T(8,128)(2,1)S(1)}, u32[]{:S(2)}, u32[]{:S(2)}) collective-permute-start(bf16[256,1792]{1,0:T(8,128)(2,1)S(1)} %bitcast_select_fusion), channel_id=1, source_target_pairs={{0,8},{8,0},{16,24},{24,16},{1,9},{9,1},{17,25},{25,17},{2,10},{10... | collective-permute-start | bytes 2752520 | tf_op jit(solution)/shard_map/ppermute | solution.py:228
  72.8 19.3 %collective-permute-start.13 = (bf16[256,1792]{1,0:T(8,128)(2,1)S(1)}, bf16[256,1792]{1,0:T(8,128)(2,1)S(1)}, u32[]{:S(2)}, u32[]{:S(2)}) collective-permute-start(bf16[256,1792]{1,0:T(8,128)(2,1)S(1)} %add_convert_fusion.3), channel_id=1, source_target_pairs={{8,16},{16,8},{9,17},{17,9},{10,18},{18,10},{11,19},{19,11},{12,20... | collective-permute-start | bytes 2752520 | tf_op jit(solution)/shard_map/ppermute | solution.py:245
  93.2 16.5 %copy-start.2 = (bf16[256,1792]{1,0:T(8,128)(2,1)}, bf16[256,1792]{1,0:T(8,128)(2,1)S(1)}, u32[]{:S(2)}) copy-start(bf16[256,1792]{1,0:T(8,128)(2,1)S(1)} %add_convert_fusion.2.refs_0_) | copy-start | bytes 2752516
  93.2 16.5 %collective-permute-start.16 = (bf16[256,1792]{1,0:T(8,128)(2,1)S(1)}, bf16[256,1792]{1,0:T(8,128)(2,1)}, u32[]{:S(2)}, u32[]{:S(2)}) collective-permute-start(bf16[256,1792]{1,0:T(8,128)(2,1)S(1)} %add_convert_fusion.1), channel_id=1, source_target_pairs={{8,16},{16,8},{9,17},{17,9},{10,18},{18,10},{11,19},{19,11},{12,20... | collective-permute-start | bytes 2752520 | tf_op jit(solution)/shard_map/ppermute | solution.py:245
  94.8 23.3 %collective-permute-start.15 = (bf16[256,1792]{1,0:T(8,128)(2,1)S(1)}, bf16[256,1792]{1,0:T(8,128)(2,1)}, u32[]{:S(2)}, u32[]{:S(2)}) collective-permute-start(bf16[256,1792]{1,0:T(8,128)(2,1)S(1)} %add_convert_fusion.2.refs_0_), channel_id=1, source_target_pairs={{8,0},{16,24},{9,1},{17,25},{10,2},{18,26},{11,3},{19,27},{12,4},{... | collective-permute-start | bytes 2752520 | tf_op jit(solution)/shard_map/ppermute | solution.py:251
  111.1 12.2 %copy-start.3 = (bf16[256,1792]{1,0:T(8,128)(2,1)}, bf16[256,1792]{1,0:T(8,128)(2,1)S(1)}, u32[]{:S(2)}) copy-start(bf16[256,1792]{1,0:T(8,128)(2,1)S(1)} %add_convert_fusion.refs_0_) | copy-start | bytes 2752516
  118.1 20.9 %collective-permute-start.17 = (bf16[256,1792]{1,0:T(8,128)(2,1)S(1)}, bf16[256,1792]{1,0:T(8,128)(2,1)S(1)}, u32[]{:S(2)}, u32[]{:S(2)}) collective-permute-start(bf16[256,1792]{1,0:T(8,128)(2,1)S(1)} %add_convert_fusion.refs_0_), channel_id=1, source_target_pairs={{8,0},{16,24},{9,1},{17,25},{10,2},{18,26},{11,3},{19,27},{12,4},{... | collective-permute-start | bytes 2752520 | tf_op jit(solution)/shard_map/ppermute | solution.py:251
  139.0 11.7 %copy-start.15 = (bf16[4,32,2048]{2,1,0:T(8,128)(2,1)S(1)}, bf16[4,32,2048]{2,1,0:T(8,128)(2,1)}, u32[]{:S(2)}) copy-start(bf16[4,32,2048]{2,1,0:T(8,128)(2,1)} %get-tuple-element.146) | copy-start | bytes 1572868
  139.0 11.7 %collective-permute-start.18 = (bf16[4,32,2048]{2,1,0:T(8,128)(2,1)}, bf16[4,32,2048]{2,1,0:T(8,128)(2,1)S(1)}, u32[]{:S(2)}, u32[]{:S(2)}) collective-permute-start(bf16[4,32,2048]{2,1,0:T(8,128)(2,1)} %get-tuple-element.147), channel_id=1, source_target_pairs={{0,1},{1,0},{2,3},{3,2},{4,5},{5,4},{6,7},{7,6},{8,9},{9,8},{10,11... | collective-permute-start | bytes 1572872 | tf_op jit(solution)/shard_map/ppermute | solution.py:256
  150.9 2.2 %collective-permute-start.19 = (bf16[4,32,2048]{2,1,0:T(8,128)(2,1)}, bf16[4,32,2048]{2,1,0:T(8,128)(2,1)S(1)}, u32[]{:S(2)}, u32[]{:S(2)}) collective-permute-start(bf16[4,32,2048]{2,1,0:T(8,128)(2,1)} %get-tuple-element.158), channel_id=1, source_target_pairs={{0,1},{1,0},{2,3},{3,2},{4,5},{5,4},{6,7},{7,6},{8,9},{9,8},{10,11... | collective-permute-start | bytes 1572872 | tf_op jit(solution)/shard_map/ppermute | solution.py:256
  153.3 17.1 %collective-permute-start.20 = (bf16[64,2048]{1,0:T(8,128)(2,1)S(1)}, bf16[64,2048]{1,0:T(8,128)(2,1)S(1)}, u32[]{:S(2)}, u32[]{:S(2)}) collective-permute-start(bf16[64,2048]{1,0:T(8,128)(2,1)S(1)} %pad_maximum_fusion.2), channel_id=1, source_target_pairs={{0,2},{1,3},{2,0},{3,1},{4,6},{5,7},{6,4},{7,5},{8,10},{9,11},{10,... | collective-permute-start | bytes 786440 | tf_op jit(solution)/shard_map/ppermute | solution.py:270
  154.8 15.6 %collective-permute-start.21 = (bf16[64,2048]{1,0:T(8,128)(2,1)S(1)}, bf16[64,2048]{1,0:T(8,128)(2,1)S(1)}, u32[]{:S(2)}, u32[]{:S(2)}) collective-permute-start(bf16[64,2048]{1,0:T(8,128)(2,1)S(1)} %pad_maximum_fusion.3), channel_id=1, source_target_pairs={{0,4},{1,5},{2,6},{3,7},{4,0},{5,1},{6,2},{7,3},{8,12},{9,13},{10,... | collective-permute-start | bytes 786440 | tf_op jit(solution)/shard_map/ppermute | solution.py:270
  155.6 14.8 %collective-permute-start.22 = (bf16[64,2048]{1,0:T(8,128)(2,1)S(1)}, bf16[64,2048]{1,0:T(8,128)(2,1)S(1)}, u32[]{:S(2)}, u32[]{:S(2)}) collective-permute-start(bf16[64,2048]{1,0:T(8,128)(2,1)S(1)} %pad_maximum_fusion.4), channel_id=1, source_target_pairs={{0,6},{1,7},{2,4},{3,5},{4,2},{5,3},{6,0},{7,1},{8,14},{9,15},{10,... | collective-permute-start | bytes 786440 | tf_op jit(solution)/shard_map/ppermute | solution.py:270
  (12 other events, 27.2 us)
Sparse Core Ops, SparseCore 0:
  28.3 26.1 all-gather.2
  56.3 27.8 all-gather.4
where the time goes:
time: 179 us; the launch traced here: 178 us
  waiting for transfers between devices  61.2 us (34%)
  Pallas kernels  60.2 us (34%)
  starting transfers between devices  27 us (15%)
  between operations  14.4 us (8%)
  other arithmetic  7.81 us (4%)
  local copies, waits for them, and re-layouts  7.59 us (4%)
    ppermute x2, waiting for transfers between devices, trade(): return lax.ppermute(given, axis, [(i, i ^ 1) for i in range(4)])  31.9 us
    pallas_call x2, Pallas kernels, input_grad_terms(): pl.pallas_call(body, grid=(depth // tile,), in_specs=[pl.BlockSpec((token...  21.6 us
    pallas_call x1, Pallas kernels, down_weight_grads(): pl.pallas_call(body, grid=(wide // tile,), in_specs=[one if x.ndim == 4 e...  13.6 us
    pallas_call x1, Pallas kernels, projection_grads(): pl.pallas_call(body, grid=(depth // tile,), in_specs=[pl.BlockSpec((tile,...  13.4 us
    ppermute x2, waiting for transfers between devices, sum_out(): lax.ppermute(found[-1], axis, [(k + 1, k), (size - 2 - k, size - 1 - k)])  11.8 us
    pallas_call x2, Pallas kernels, hidden_grad_terms(): pl.pallas_call(body, grid=(wide // tile,), in_specs=[pl.BlockSpec((None,...  11.5 us
    ppermute x3, waiting for transfers between devices, shards(): lax.ppermute(own, 'col', [(i, i ^ 2 * k) for i in range(n_col)])  10.8 us
    ppermute x4, starting transfers between devices, gather_near(): return [shard] + [lax.ppermute(shard, axis, pairs) for pairs in swaps]  9.36 us
  transfers between devices with their start and end apart: 25, of which 12 were waited for; matrix products, arithmetic and copies ran while one was open for 6% of the time, Pallas kernels for 34%

commit v1 on v0

--- a/solution.py
+++ b/solution.py
@@ -59,18 +59,24 @@
         grid=(wide // tile,),
         in_specs=[pl.BlockSpec((None, rows, depth), lambda i: (q, 0, 0))] * (2 * half)
         + [pl.BlockSpec((tile, depth), lambda i: (i, 0))],
-        out_specs=pl.BlockSpec((tokens, tile), lambda i: (0, i)),
-        out_shape=jax.ShapeDtypeStruct((tokens, wide), jnp.bfloat16),
-        scratch_shapes=[pltpu.VMEM((2 * half, rows, depth), jnp.bfloat16)],
+        out_specs=[
+            pl.BlockSpec((tokens, tile), lambda i: (0, i)),
+            pl.BlockSpec((2 * half, rows, depth), lambda i: (0, 0, 0)),
+        ],
+        out_shape=[
+            jax.ShapeDtypeStruct((tokens, wide), jnp.bfloat16),
+            jax.ShapeDtypeStruct((2 * half, rows, depth), jnp.bfloat16),
+        ],
         compiler_params=params(),
         cost_estimate=cost(2 * tokens * depth * wide, 2 * (down.size + tokens * depth)),
         name="hidden_grad_terms",
     )(*pieces, *others, down)
 
 
-def down_weight_grads(saved, places, grad, axis, scale):
+def down_weight_grads(saved, places, grads, axis, scale):
     blocks, _, _, wide = saved[0][0].shape
-    cols, chunks, rows, depth = grad.shape
+    cols, rows, depth = grads[0].shape
+    chunks = len(grads)
     tokens = chunks * cols * rows
     tile = tile_of(wide, 256)
     flat = [x for shard in saved for x in shard]
@@ -78,7 +84,8 @@
 
     def body(*refs):
         saved_refs = list(refs[:n])
-        grad_ref, out_ref, by_gate_ref, by_up_ref, hidden_ref = refs[n:]
+        grad_refs, refs = refs[n : n + chunks], refs[n + chunks :]
+        out_ref, by_gate_ref, by_up_ref, hidden_ref = refs
         for k, (shard, there) in enumerate(places(lax.axis_index(axis))):
             pair = [saved_refs.pop(0) for _ in saved[k]]
             gate_ref, up_ref = pair if len(pair) == 2 else (pair[0].at[0], pair[0].at[1])
@@ -95,9 +102,11 @@
                 by_gate_ref[to] = (up_val * slope).astype(jnp.bfloat16)
                 by_up_ref[to] = silu.astype(jnp.bfloat16)
 
-        left = hidden_ref[...].reshape(tokens, tile)
-        right = grad_ref[...].reshape(tokens, depth)
-        out_ref[...] = scale * dot(left, right, ((0,), (0,)))
+        res = 0.0
+        for q in range(chunks):
+            left = hidden_ref[:, q].reshape(cols * rows, tile)
+            res += dot(left, grad_refs[q][...].reshape(cols * rows, depth), ((0,), (0,)))
+        out_ref[...] = scale * res
 
     one = pl.BlockSpec((blocks, chunks, rows, tile), lambda i: (0, 0, 0, i))
     two = pl.BlockSpec((2, blocks, chunks, rows, tile), lambda i: (0, 0, 0, 0, i))
@@ -107,14 +116,14 @@
         body,
         grid=(wide // tile,),
         in_specs=[one if x.ndim == 4 else two for x in flat]
-        + [pl.BlockSpec((cols, chunks, rows, depth), lambda i: (0, 0, 0, 0))],
+        + [pl.BlockSpec((cols, rows, depth), lambda i: (0, 0, 0))] * chunks,
         out_specs=[pl.BlockSpec((tile, depth), lambda i: (i, 0)), factor, factor],
         out_shape=[jax.ShapeDtypeStruct((wide, depth), jnp.float32), factors, factors],
         scratch_shapes=[pltpu.VMEM((cols, chunks, rows, tile), jnp.bfloat16)],
         compiler_params=params(),
         cost_estimate=cost(2 * tokens * wide * depth, 4 * wide * depth),
         name="down_weight_grads",
-    )(*flat, grad)
+    )(*flat, *grads)
 
 
 def input_grad_terms(q, sums, by_gate, by_up, gate_weight, up_weight, axes, made):
@@ -195,6 +204,43 @@
     )(inputs, gate_grad, up_grad)
 
 
+def turned(pieces, others, axis):
+    half = len(pieces)
+    rows, depth = pieces[0].shape
+    tile = tile_of(depth, 512)
+
+    def body(*refs):
+        out_ref, whole_ref = refs[2 * half :]
+        here = lax.axis_index(axis)
+        for k in range(half):
+            whole_ref[here ^ (2 * k)] = refs[k][...]
+            whole_ref[here ^ (2 * k + 1)] = refs[half + k][...]
+        out_ref[...] = whole_ref[...].reshape(2 * half * rows, tile).T
+
+    tokens = 2 * half * rows
+    return pl.pallas_call(
+        body,
+        grid=(depth // tile,),
+        in_specs=[pl.BlockSpec((rows, tile), lambda i: (0, i))] * (2 * half),
+        out_specs=pl.BlockSpec((tile, tokens), lambda i: (i, 0)),
+        out_shape=jax.ShapeDtypeStruct((depth, tokens), jnp.bfloat16),
+        scratch_shapes=[pltpu.VMEM((2 * half, rows, tile), jnp.bfloat16)],
+        compiler_params=params(),
+        cost_estimate=cost(1, 4 * depth * tokens),
+        name="turned",
+    )(*pieces, *others)
+
+
+def gather_parity(own, axis, size):
+    return [own] + [
+        lax.ppermute(own, axis, [(i, i ^ (2 * k)) for i in range(size)]) for k in range(1, size // 2)
+    ]
+
+
+def gather_others(pieces, axis, size):
+    return [lax.ppermute(x, axis, [(i, i ^ 1) for i in range(size)]) for x in pieces]
+
+
 def gather_places(size):
     def places(here):
         if size != 4:
@@ -290,20 +336,15 @@
         view = (row_tokens // block, CHUNKS, rows, wide)
         gates = gather_near(gate_saved.reshape(view), "row", n_row)
         up_saved = up_saved.reshape(view)
-        own = out_grad.reshape(CHUNKS, rows, depth)
-        pieces = [own] + [
-            lax.ppermute(own, "col", [(i, i ^ (2 * k)) for i in range(n_col)])
-            for k in range(1, n_col // 2)
-        ]
-        pieces, gates, up_saved, out_grad, layer_input = hold(
-            pieces, gates, up_saved, out_grad, layer_input
+        pieces = gather_parity(out_grad.reshape(CHUNKS, rows, depth), "col", n_col)
+        pieces, gates, up_saved, layer_input = hold(pieces, gates, up_saved, layer_input)
+        ups = gather_near(up_saved, "row", n_row)
+        others = gather_others(pieces, "col", n_col)
+        first, grad = hidden_grad_terms(0, pieces, others, "col", down_weight)
+        grads = [grad]
+        first, gates, ups, pieces, others, layer_input = hold(
+            first, gates, ups, pieces, others, layer_input
         )
-        ups = gather_near(up_saved, "row", n_row)
-        others = [lax.ppermute(x, "col", [(i, i ^ 1) for i in range(n_col)]) for x in pieces]
-        grad = lax.all_gather(out_grad, "col", axis=0, tiled=True)
-        inputs = lax.all_gather(layer_input, "col", axis=0, tiled=True)
-        first = hidden_grad_terms(0, pieces, others, "col", down_weight)
-        first, gates, ups, pieces, others = hold(first, gates, ups, pieces, others)
 
         line = n_row == 4 and 2 * row_tokens * CHUNKS == tokens
         saved = [list(pair) for pair in zip(gates, ups)]
@@ -314,8 +355,9 @@
             saved += [[passed], [got.reshape(passed.shape)]]
         else:
             first = sum_in(first, "row", n_row)
-        second = hidden_grad_terms(1, pieces, others, "col", down_weight)
-        first, second, saved = hold(first, second, saved)
+        second, grad = hidden_grad_terms(1, pieces, others, "col", down_weight)
+        grads.append(grad)
+        first, second, saved, layer_input = hold(first, second, saved, layer_input)
 
         if line:
             got = trade(second, saved[3][0], "row")
@@ -324,21 +366,22 @@
         else:
             second = sum_in(second, "row", n_row)
         first = sum_swap(first, "row", n_row)
-        first, second, grad, saved = hold(first, second, grad, saved)
+        inputs = gather_parity(layer_input, "col", n_col)
+        first, second, saved, inputs = hold(first, second, saved, inputs)
 
         first = sum_out(first, "row", n_row)
         second = sum_swap(second, "row", n_row)
-        grad = grad.reshape(n_col, CHUNKS, rows, depth)
         down_weight_grad, *factors = down_weight_grads(
-            saved, gather_places(n_row), grad, "row", scale
+            saved, gather_places(n_row), grads, "row", scale
         )
-        first, second, down_weight_grad, factors, inputs = hold(
-            first, second, down_weight_grad, factors, inputs
+        other_inputs = gather_others(inputs, "col", n_col)
+        first, second, down_weight_grad, factors, other_inputs = hold(
+            first, second, down_weight_grad, factors, other_inputs
         )
 
         second = sum_out(second, "row", n_row)
         *made, keep, send = input_grad_terms(0, first, *factors, *weights, ())
-        inputs = inputs.T
+        inputs = turned(inputs, other_inputs, "col")
         second, made, keep, send, inputs = hold(second, made, keep, send, inputs)
 
         early = scatter_halves(keep, send, "col", n_col)

time: 179 us -> 167 us (0.933)
  between operations: 14.4 us -> 1.11 us
  starting transfers between devices: 27 us -> 32.1 us
  Pallas kernels: 60.2 us -> 64.6 us
  local copies, waits for them, and re-layouts: 7.59 us -> 3.55 us
  waiting for transfers between devices: 61.2 us -> 58.8 us
  other arithmetic: 7.81 us -> 6.01 us
    ppermute x7 -> x14, starting transfers between devices: 4.07 us -> 8.77 us  [the longest x6 7.04 us: gather_parity(): lax.ppermute(own, axis, [(i, i ^ 2 * k) for i in range(size)])]
    ppermute x2, waiting for transfers between devices: 31.9 us -> 27.5 us  [trade(): return lax.ppermute(given, axis, [(i, i ^ 1) for i in range(4)])]
    pallas_call x0 -> x1, Pallas kernels: none -> 4.22 us  [turned(): pl.pallas_call(body, grid=(depth // tile,), in_specs=[pl.BlockSpec((rows,...]
    optimization_barrier x1 -> x0, local copies, waits for them, and re-layouts: 3.93 us -> none  [hold(): return lax.optimization_barrier(values)]
    ppermute x2, waiting for transfers between devices: 11.8 us -> 14.7 us  [sum_out(): lax.ppermute(found[-1], axis, [(k + 1, k), (size - 2 - k, size - 1 - k)])]
    ppermute x7 -> x14, waiting for transfers between devices: 12.5 us -> 12.5 us  [the longest x6 10.8 us: gather_parity(): lax.ppermute(own, axis, [(i, i ^ 2 * k) for i in range(size)])]
  transfers between devices with their start and end apart: 25 -> 30, of which waited for: 12 -> 12; matrix products, arithmetic and copies ran while one was open for 6% -> 3% of each run, Pallas kernels for 34% -> 39%
where the time goes in v1:
time: 167 us; the launch traced here: 166 us
  Pallas kernels  64.6 us (39%)
  waiting for transfers between devices  58.8 us (35%)
  starting transfers between devices  32.1 us (19%)
  other arithmetic  6.01 us (4%)
  local copies, waits for them, and re-layouts  3.55 us (2%)
    ppermute x2, waiting for transfers between devices, trade(): return lax.ppermute(given, axis, [(i, i ^ 1) for i in range(4)])  27.5 us
    pallas_call x2, Pallas kernels, input_grad_terms(): pl.pallas_call(body, grid=(depth // tile,), in_specs=[pl.BlockSpec((token...  21.7 us
    ppermute x2, waiting for transfers between devices, sum_out(): lax.ppermute(found[-1], axis, [(k + 1, k), (size - 2 - k, size - 1 - k)])  14.7 us
    pallas_call x1, Pallas kernels, down_weight_grads(): pl.pallas_call(body, grid=(wide // tile,), in_specs=[one if x.ndim == 4 e...  13.5 us
    pallas_call x1, Pallas kernels, projection_grads(): pl.pallas_call(body, grid=(depth // tile,), in_specs=[pl.BlockSpec((tile,...  13.4 us
    pallas_call x2, Pallas kernels, hidden_grad_terms(): pl.pallas_call(body, grid=(wide // tile,), in_specs=[pl.BlockSpec((None,...  11.7 us
    ppermute x6, waiting for transfers between devices, gather_parity(): lax.ppermute(own, axis, [(i, i ^ 2 * k) for i in range(size)])  10.8 us
    ppermute x4, starting transfers between devices, gather_near(): return [shard] + [lax.ppermute(shard, axis, pairs) for pairs in swaps]  9.36 us
  transfers between devices with their start and end apart: 30, of which 12 were waited for; matrix products, arithmetic and copies ran while one was open for 3% of the time, Pallas kernels for 39%

profile of v1, /device:TPU:0, one launch (start us, length us, event | category | flops | bytes accessed | tf_op | source)
XLA Modules:
  0.0 166.1 jit_solution(334889876000916379)
XLA Ops:
  1.3 5.9 %collective-permute-start.3 = (bf16[2,2,32,1792]{3,2,1,0:T(8,128)(2,1)}, bf16[2,2,32,1792]{3,2,1,0:T(8,128)(2,1)S(1)}, u32[]{:S(2)}, u32[]{:S(2)}) collective-permute-start(bf16[2,2,32,1792]{3,2,1,0:T(8,128)(2,1)} %bitcast.47), channel_id=1, source_target_pairs={{0,8},{8,0},{16,24},{24,16},{1,9},{9,1},{17,25},{25,17},{2,10},{10... | collective-permute-start | bytes 1376264 | tf_op jit(solution)/shard_map/ppermute | solution.py:267
  7.2 2.4 %collective-permute-start.2 = (bf16[2,32,2048]{2,1,0:T(8,128)(2,1)}, bf16[2,32,2048]{2,1,0:T(8,128)(2,1)S(1)}, u32[]{:S(2)}, u32[]{:S(2)}) collective-permute-start(bf16[2,32,2048]{2,1,0:T(8,128)(2,1)} %bitcast.33), channel_id=1, source_target_pairs={{0,6},{1,7},{2,4},{3,5},{4,2},{5,3},{6,0},{7,1},{8,14},{9,15},{10,... | collective-permute-start | bytes 786440 | tf_op jit(solution)/shard_map/ppermute | solution.py:236
  10.7 6.9 %collective-permute-done.2.refs_3_ = bf16[2,32,2048]{2,1,0:T(8,128)(2,1)S(1)} collective-permute-done((bf16[2,32,2048]{2,1,0:T(8,128)(2,1)}, bf16[2,32,2048]{2,1,0:T(8,128)(2,1)S(1)}, u32[]{:S(2)}, u32[]{:S(2)}) %collective-permute-start.2) | collective-permute-done | bytes 262176 | tf_op jit(solution)/shard_map/ppermute | solution.py:236
  17.6 3.8 %collective-permute-done.1.refs_2_ = bf16[2,32,2048]{2,1,0:T(8,128)(2,1)S(1)} collective-permute-done((bf16[2,32,2048]{2,1,0:T(8,128)(2,1)}, bf16[2,32,2048]{2,1,0:T(8,128)(2,1)S(1)}, u32[]{:S(2)}, u32[]{:S(2)}) %collective-permute-start.1) | collective-permute-done | bytes 262176 | tf_op jit(solution)/shard_map/ppermute | solution.py:236
  22.3 2.1 %collective-permute-start.9 = (bf16[2,2,32,1792]{3,2,1,0:T(8,128)(2,1)}, bf16[2,2,32,1792]{3,2,1,0:T(8,128)(2,1)}, u32[]{:S(2)}, u32[]{:S(2)}) collective-permute-start(bf16[2,2,32,1792]{3,2,1,0:T(8,128)(2,1)} %bitcast.44), channel_id=1, source_target_pairs={{0,8},{8,0},{16,24},{24,16},{1,9},{9,1},{17,25},{25,17},{2,10},{10... | collective-permute-start | bytes 1376264 | tf_op jit(solution)/shard_map/ppermute | solution.py:267
  25.0 0.9 collective-permute-done.6.refs_5_
  27.7 5.9 %hidden_grad_terms.2 = (bf16[256,1792]{1,0:T(8,128)(2,1)}, bf16[8,32,2048]{2,1,0:T(8,128)(2,1)}) custom-call(bf16[2,32,2048]{2,1,0:T(8,128)(2,1)} %bitcast.37, bf16[2,32,2048]{2,1,0:T(8,128)(2,1)} %copy-done.6, bf16[2,32,2048]{2,1,0:T(8,128)(2,1)} %copy-done.5, bf16[2,32,2048]{2,1,0:T(8,128)(2,1)} %copy-done.4, bf16[2,32,2048]{2,1,0:T(8,128)(2,1)} %copy-done.7, ...), custom_call_target="tpu_custom_call" | custom-call | flops 1879048192 | bytes 8388608 | tf_op jit(solution)/shard_map/hidden_grad_terms/pallas_call | solution.py:57
  33.6 2.0 %collective-permute-done.9.refs_3_ = bf16[2,2,32,1792]{3,2,1,0:T(8,128)(2,1)} collective-permute-done((bf16[2,2,32,1792]{3,2,1,0:T(8,128)(2,1)}, bf16[2,2,32,1792]{3,2,1,0:T(8,128)(2,1)}, u32[]{:S(2)}, u32[]{:S(2)}) %collective-permute-start.9) | collective-permute-done | bytes 458784 | tf_op jit(solution)/shard_map/ppermute | solution.py:267
  35.9 1.9 %collective-permute-start.11 = (bf16[256,1792]{1,0:T(8,128)(2,1)S(1)}, bf16[256,1792]{1,0:T(8,128)(2,1)}, u32[]{:S(2)}, u32[]{:S(2)}) collective-permute-start(bf16[256,1792]{1,0:T(8,128)(2,1)S(1)} %bitcast_select_fusion.1), channel_id=1, source_target_pairs={{0,8},{8,0},{16,24},{24,16},{1,9},{9,1},{17,25},{25,17},{2,10},{10... | collective-permute-start | bytes 2752520 | tf_op jit(solution)/shard_map/ppermute | solution.py:274
  37.8 1.2 pad_maximum_fusion.1
  39.8 5.9 %hidden_grad_terms.3 = (bf16[256,1792]{1,0:T(8,128)(2,1)}, bf16[8,32,2048]{2,1,0:T(8,128)(2,1)}) custom-call(bf16[2,32,2048]{2,1,0:T(8,128)(2,1)} %bitcast.38, bf16[2,32,2048]{2,1,0:T(8,128)(2,1)} %copy-done.6, bf16[2,32,2048]{2,1,0:T(8,128)(2,1)} %copy-done.5, bf16[2,32,2048]{2,1,0:T(8,128)(2,1)} %copy-done.4, bf16[2,32,2048]{2,1,0:T(8,128)(2,1)} %copy-done.7, ...), custom_call_target="tpu_custom_call" | custom-call | flops 1879048192 | bytes 8388608 | tf_op jit(solution)/shard_map/hidden_grad_terms/pallas_call | solution.py:57
  45.7 12.6 %collective-permute-done.11 = bf16[256,1792]{1,0:T(8,128)(2,1)} collective-permute-done((bf16[256,1792]{1,0:T(8,128)(2,1)S(1)}, bf16[256,1792]{1,0:T(8,128)(2,1)}, u32[]{:S(2)}, u32[]{:S(2)}) %collective-permute-start.11) | collective-permute-done | bytes 917536 | tf_op jit(solution)/shard_map/ppermute | solution.py:274
  58.3 1.4 add_convert_fusion.3
  59.9 3.4 %collective-permute-start.14 = (bf16[256,1792]{1,0:T(8,128)(2,1)S(1)}, bf16[256,1792]{1,0:T(8,128)(2,1)S(1)}, u32[]{:S(2)}, u32[]{:S(2)}) collective-permute-start(bf16[256,1792]{1,0:T(8,128)(2,1)S(1)} %bitcast_select_fusion), channel_id=1, source_target_pairs={{0,8},{8,0},{16,24},{24,16},{1,9},{9,1},{17,25},{25,17},{2,10},{10... | collective-permute-start | bytes 2752520 | tf_op jit(solution)/shard_map/ppermute | solution.py:274
  64.0 1.7 %collective-permute-start.17 = (bf16[64,2048]{1,0:T(8,128)(2,1)S(1)}, bf16[64,2048]{1,0:T(8,128)(2,1)}, u32[]{:S(2)}, u32[]{:S(2)}) collective-permute-start(bf16[64,2048]{1,0:T(8,128)(2,1)S(1)} %copy-done.21), channel_id=1, source_target_pairs={{0,6},{1,7},{2,4},{3,5},{4,2},{5,3},{6,0},{7,1},{8,14},{9,15},{10,... | collective-permute-start | bytes 786440 | tf_op jit(solution)/shard_map/ppermute | solution.py:236
  65.7 1.3 collective-permute-start.16
  67.5 14.9 %collective-permute-done.14 = bf16[256,1792]{1,0:T(8,128)(2,1)S(1)} collective-permute-done((bf16[256,1792]{1,0:T(8,128)(2,1)S(1)}, bf16[256,1792]{1,0:T(8,128)(2,1)S(1)}, u32[]{:S(2)}, u32[]{:S(2)}) %collective-permute-start.14) | collective-permute-done | bytes 917536 | tf_op jit(solution)/shard_map/ppermute | solution.py:274
  84.2 1.3 collective-permute-start.18
  86.2 13.5 %down_weight_grads.1 = (f32[1792,2048]{1,0:T(8,128)}, bf16[8,2,32,1792]{3,2,1,0:T(8,128)(2,1)}, bf16[8,2,32,1792]{3,2,1,0:T(8,128)(2,1)}) custom-call(bf16[2,2,32,1792]{3,2,1,0:T(8,128)(2,1)} %bitcast.48, bf16[2,2,32,1792]{3,2,1,0:T(8,128)(2,1)} %bitcast.45, bf16[2,2,32,1792]{3,2,1,0:T(8,128)(2,1)} %copy-done.19, ...), custom_call_target="tpu_custom_call" | custom-call | flops 3758096384 | bytes 14680064 | tf_op jit(solution)/shard_map/down_weight_grads/pallas_call | solution.py:115
  99.7 0.9 copy-done.14
  101.1 1.4 add_convert_fusion.refs_0_
  102.6 6.0 %collective-permute-done.18.refs_1_ = bf16[256,1792]{1,0:T(8,128)(2,1)S(1)} collective-permute-done((bf16[256,1792]{1,0:T(8,128)(2,1)S(1)}, bf16[256,1792]{1,0:T(8,128)(2,1)S(1)}, u32[]{:S(2)}, u32[]{:S(2)}) %collective-permute-start.18) | collective-permute-done | bytes 917536 | tf_op jit(solution)/shard_map/ppermute | solution.py:297
  108.6 1.5 collective-permute-start.24
  110.1 4.2 %turned.1.inputs_ref = bf16[2048,512]{1,0:T(8,128)(2,1)} custom-call(bf16[64,2048]{1,0:T(8,128)(2,1)} %refs_0_, bf16[64,2048]{1,0:T(8,128)(2,1)} %collective-permute-done.15.refs_1_, bf16[64,2048]{1,0:T(8,128)(2,1)} %collective-permute-done.16.refs_2_, bf16[64,2048]{1,0:T(8,128)(2,1)} %collective-permute-done.17.refs_3_, ...), custom_call_target="tpu_custom_call" | custom-call | flops 1 | bytes 4194304 | tf_op jit(solution)/shard_map/turned/pallas_call | solution.py:221
  114.3 10.9 %input_grad_terms.2 = (bf16[8,2,32,1792]{3,2,1,0:T(8,128)(2,1)}, bf16[8,2,32,1792]{3,2,1,0:T(8,128)(2,1)}, bf16[4,32,2048]{2,1,0:T(8,128)(2,1)}, bf16[4,32,2048]{2,1,0:T(8,128)(2,1)}) custom-call(bf16[256,1792]{1,0:T(8,128)(2,1)} %copy-done.2, bf16[256,1792]{1,0:T(8,128)(2,1)} %copy-done.13, bf16[8,2,32,1792]{3,2,1,0:T(8,128)(2,1)} %get-tuple-element.158.refs_2_, ...), custom_call_target="tpu_custom_call" | custom-call | flops 3758096384 | bytes 14680064 | tf_op jit(solution)/shard_map/input_grad_terms/pallas_call | solution.py:168
  125.2 8.6 %collective-permute-done.24.refs_1_ = bf16[256,1792]{1,0:T(8,128)(2,1)S(1)} collective-permute-done((bf16[256,1792]{1,0:T(8,128)(2,1)S(1)}, bf16[256,1792]{1,0:T(8,128)(2,1)S(1)}, u32[]{:S(2)}, u32[]{:S(2)}) %collective-permute-start.24) | collective-permute-done | bytes 917536 | tf_op jit(solution)/shard_map/ppermute | solution.py:297
  133.8 0.9 copy-done.15
  134.7 10.8 %input_grad_terms.3 = (bf16[8,2,32,1792]{3,2,1,0:T(8,128)(2,1)}, bf16[8,2,32,1792]{3,2,1,0:T(8,128)(2,1)}, bf16[4,32,2048]{2,1,0:T(8,128)(2,1)}, bf16[4,32,2048]{2,1,0:T(8,128)(2,1)}) custom-call(bf16[256,1792]{1,0:T(8,128)(2,1)} %copy-done.3, bf16[256,1792]{1,0:T(8,128)(2,1)} %copy-done.15, ...), custom_call_target="tpu_custom_call", output_to_operand_aliasing={{0}: (6, {}), {1}: (7, {})} | custom-call | flops 3758096384 | bytes 14680064 | tf_op jit(solution)/shard_map/input_grad_terms/pallas_call | solution.py:168
  145.9 2.0 %collective-permute-done.26 = bf16[4,32,2048]{2,1,0:T(8,128)(2,1)S(1)} collective-permute-done((bf16[4,32,2048]{2,1,0:T(8,128)(2,1)}, bf16[4,32,2048]{2,1,0:T(8,128)(2,1)S(1)}, u32[]{:S(2)}, u32[]{:S(2)}) %collective-permute-start.26) | collective-permute-done | bytes 524320 | tf_op jit(solution)/shard_map/ppermute | solution.py:302
  148.1 1.6 collective-permute-start.27
  150.5 1.3 collective-permute-start.29
  151.8 13.4 %projection_grads.1 = (f32[2048,1792]{1,0:T(8,128)}, f32[2048,1792]{1,0:T(8,128)}) custom-call(bf16[2048,512]{1,0:T(8,128)(2,1)} %turned.1.inputs_ref, bf16[512,1792]{1,0:T(8,128)(2,1)} %bitcast.31, bf16[512,1792]{1,0:T(8,128)(2,1)} %bitcast.32), custom_call_target="tpu_custom_call" | custom-call | flops 7516192768 | bytes 29360128 | tf_op jit(solution)/shard_map/projection_grads/pallas_call | solution.py:195
  (97 shorter events, 12.3 us)
Async XLA Ops:
  0.6 20.9 %collective-permute-start.4 = (bf16[2,2,32,1792]{3,2,1,0:T(8,128)(2,1)}, bf16[2,2,32,1792]{3,2,1,0:T(8,128)(2,1)S(1)}, u32[]{:S(2)}, u32[]{:S(2)}) collective-permute-start(bf16[2,2,32,1792]{3,2,1,0:T(8,128)(2,1)} %bitcast.46), channel_id=1, source_target_pairs={{8,16},{16,8},{9,17},{17,9},{10,18},{18,10},{11,19},{19,11},{12,20... | collective-permute-start | bytes 1376264 | tf_op jit(solution)/shard_map/ppermute | solution.py:267
  1.3 20.2 %collective-permute-start.3 = (bf16[2,2,32,1792]{3,2,1,0:T(8,128)(2,1)}, bf16[2,2,32,1792]{3,2,1,0:T(8,128)(2,1)S(1)}, u32[]{:S(2)}, u32[]{:S(2)}) collective-permute-start(bf16[2,2,32,1792]{3,2,1,0:T(8,128)(2,1)} %bitcast.47), channel_id=1, source_target_pairs={{0,8},{8,0},{16,24},{24,16},{1,9},{9,1},{17,25},{25,17},{2,10},{10... | collective-permute-start | bytes 1376264 | tf_op jit(solution)/shard_map/ppermute | solution.py:267
  7.2 10.4 %collective-permute-start.2 = (bf16[2,32,2048]{2,1,0:T(8,128)(2,1)}, bf16[2,32,2048]{2,1,0:T(8,128)(2,1)S(1)}, u32[]{:S(2)}, u32[]{:S(2)}) collective-permute-start(bf16[2,32,2048]{2,1,0:T(8,128)(2,1)} %bitcast.33), channel_id=1, source_target_pairs={{0,6},{1,7},{2,4},{3,5},{4,2},{5,3},{6,0},{7,1},{8,14},{9,15},{10,... | collective-permute-start | bytes 786440 | tf_op jit(solution)/shard_map/ppermute | solution.py:236
  9.7 11.8 %collective-permute-start.1 = (bf16[2,32,2048]{2,1,0:T(8,128)(2,1)}, bf16[2,32,2048]{2,1,0:T(8,128)(2,1)S(1)}, u32[]{:S(2)}, u32[]{:S(2)}) collective-permute-start(bf16[2,32,2048]{2,1,0:T(8,128)(2,1)} %bitcast.34), channel_id=1, source_target_pairs={{0,4},{1,5},{2,6},{3,7},{4,0},{5,1},{6,2},{7,3},{8,12},{9,13},{10,... | collective-permute-start | bytes 786440 | tf_op jit(solution)/shard_map/ppermute | solution.py:236
  10.2 11.4 %collective-permute-start = (bf16[2,32,2048]{2,1,0:T(8,128)(2,1)}, bf16[2,32,2048]{2,1,0:T(8,128)(2,1)S(1)}, u32[]{:S(2)}, u32[]{:S(2)}) collective-permute-start(bf16[2,32,2048]{2,1,0:T(8,128)(2,1)} %bitcast.35), channel_id=1, source_target_pairs={{0,2},{1,3},{2,0},{3,1},{4,6},{5,7},{6,4},{7,5},{8,10},{9,11},{10,... | collective-permute-start | bytes 786440 | tf_op jit(solution)/shard_map/ppermute | solution.py:236
  21.6 3.4 %collective-permute-start.5 = (bf16[2,32,2048]{2,1,0:T(8,128)(2,1)}, bf16[2,32,2048]{2,1,0:T(8,128)(2,1)S(1)}, u32[]{:S(2)}, u32[]{:S(2)}) collective-permute-start(bf16[2,32,2048]{2,1,0:T(8,128)(2,1)} %bitcast.36), channel_id=1, source_target_pairs={{0,1},{1,0},{2,3},{3,2},{4,5},{5,4},{6,7},{7,6},{8,9},{9,8},{10,11... | collective-permute-start | bytes 786440 | tf_op jit(solution)/shard_map/ppermute | solution.py:241
  21.6 12.0 %collective-permute-start.10 = (bf16[2,2,32,1792]{3,2,1,0:T(8,128)(2,1)}, bf16[2,2,32,1792]{3,2,1,0:T(8,128)(2,1)S(1)}, u32[]{:S(2)}, u32[]{:S(2)}) collective-permute-start(bf16[2,2,32,1792]{3,2,1,0:T(8,128)(2,1)} %bitcast.43), channel_id=1, source_target_pairs={{8,16},{16,8},{9,17},{17,9},{10,18},{18,10},{11,19},{19,11},{12,20... | collective-permute-start | bytes 1376264 | tf_op jit(solution)/shard_map/ppermute | solution.py:267
  22.3 13.3 %collective-permute-start.9 = (bf16[2,2,32,1792]{3,2,1,0:T(8,128)(2,1)}, bf16[2,2,32,1792]{3,2,1,0:T(8,128)(2,1)}, u32[]{:S(2)}, u32[]{:S(2)}) collective-permute-start(bf16[2,2,32,1792]{3,2,1,0:T(8,128)(2,1)} %bitcast.44), channel_id=1, source_target_pairs={{0,8},{8,0},{16,24},{24,16},{1,9},{9,1},{17,25},{25,17},{2,10},{10... | collective-permute-start | bytes 1376264 | tf_op jit(solution)/shard_map/ppermute | solution.py:267
  24.4 1.5 collective-permute-start.6
  24.4 1.9 %collective-permute-start.7 = (bf16[2,32,2048]{2,1,0:T(8,128)(2,1)S(1)}, bf16[2,32,2048]{2,1,0:T(8,128)(2,1)S(1)}, u32[]{:S(2)}, u32[]{:S(2)}) collective-permute-start(bf16[2,32,2048]{2,1,0:T(8,128)(2,1)S(1)} %collective-permute-done.1.refs_2_), channel_id=1, source_target_pairs={{0,1},{1,0},{2,3},{3,2},{4,5},{5,4},{6,7},{7,6},{8,9},{9,8},{10,11... | collective-permute-start | bytes 786440 | tf_op jit(solution)/shard_map/ppermute | solution.py:241
  24.9 1.8 %collective-permute-start.8 = (bf16[2,32,2048]{2,1,0:T(8,128)(2,1)S(1)}, bf16[2,32,2048]{2,1,0:T(8,128)(2,1)S(1)}, u32[]{:S(2)}, u32[]{:S(2)}) collective-permute-start(bf16[2,32,2048]{2,1,0:T(8,128)(2,1)S(1)} %collective-permute-done.2.refs_3_), channel_id=1, source_target_pairs={{0,1},{1,0},{2,3},{3,2},{4,5},{5,4},{6,7},{7,6},{8,9},{9,8},{10,11... | collective-permute-start | bytes 786440 | tf_op jit(solution)/shard_map/ppermute | solution.py:241
  35.9 22.3 %collective-permute-start.11 = (bf16[256,1792]{1,0:T(8,128)(2,1)S(1)}, bf16[256,1792]{1,0:T(8,128)(2,1)}, u32[]{:S(2)}, u32[]{:S(2)}) collective-permute-start(bf16[256,1792]{1,0:T(8,128)(2,1)S(1)} %bitcast_select_fusion.1), channel_id=1, source_target_pairs={{0,8},{8,0},{16,24},{24,16},{1,9},{9,1},{17,25},{25,17},{2,10},{10... | collective-permute-start | bytes 2752520 | tf_op jit(solution)/shard_map/ppermute | solution.py:274
  39.1 20.6 %collective-permute-start.12 = (bf16[2,2,2,32,1792]{4,3,2,1,0:T(8,128)(2,1)S(1)}, bf16[2,2,2,32,1792]{4,3,2,1,0:T(8,128)(2,1)S(1)}, u32[]{:S(2)}, u32[]{:S(2)}) collective-permute-start(bf16[2,2,2,32,1792]{4,3,2,1,0:T(8,128)(2,1)S(1)} %pad_maximum_fusion.1), channel_id=1, source_target_pairs={{8,16},{16,8},{9,17},{17,9},{10,18},{18,10},{11,19},{19,11},{12,20... | collective-permute-start | bytes 2752520 | tf_op jit(solution)/shard_map/ppermute | solution.py:353
  59.7 23.0 %copy-start.11 = (bf16[2,2,2,32,1792]{4,3,2,1,0:T(8,128)(2,1)}, bf16[2,2,2,32,1792]{4,3,2,1,0:T(8,128)(2,1)S(1)}, u32[]{:S(2)}) copy-start(bf16[2,2,2,32,1792]{4,3,2,1,0:T(8,128)(2,1)S(1)} %collective-permute-done.12.refs_6_) | copy-start | bytes 2752516
  59.9 22.6 %collective-permute-start.14 = (bf16[256,1792]{1,0:T(8,128)(2,1)S(1)}, bf16[256,1792]{1,0:T(8,128)(2,1)S(1)}, u32[]{:S(2)}, u32[]{:S(2)}) collective-permute-start(bf16[256,1792]{1,0:T(8,128)(2,1)S(1)} %bitcast_select_fusion), channel_id=1, source_target_pairs={{0,8},{8,0},{16,24},{24,16},{1,9},{9,1},{17,25},{25,17},{2,10},{10... | collective-permute-start | bytes 2752520 | tf_op jit(solution)/shard_map/ppermute | solution.py:274
  63.3 19.5 %collective-permute-start.13 = (bf16[256,1792]{1,0:T(8,128)(2,1)S(1)}, bf16[256,1792]{1,0:T(8,128)(2,1)S(1)}, u32[]{:S(2)}, u32[]{:S(2)}) collective-permute-start(bf16[256,1792]{1,0:T(8,128)(2,1)S(1)} %add_convert_fusion.3), channel_id=1, source_target_pairs={{8,16},{16,8},{9,17},{17,9},{10,18},{18,10},{11,19},{19,11},{12,20... | collective-permute-start | bytes 2752520 | tf_op jit(solution)/shard_map/ppermute | solution.py:291
  64.0 19.5 %collective-permute-start.17 = (bf16[64,2048]{1,0:T(8,128)(2,1)S(1)}, bf16[64,2048]{1,0:T(8,128)(2,1)}, u32[]{:S(2)}, u32[]{:S(2)}) collective-permute-start(bf16[64,2048]{1,0:T(8,128)(2,1)S(1)} %copy-done.21), channel_id=1, source_target_pairs={{0,6},{1,7},{2,4},{3,5},{4,2},{5,3},{6,0},{7,1},{8,14},{9,15},{10,... | collective-permute-start | bytes 786440 | tf_op jit(solution)/shard_map/ppermute | solution.py:236
  65.7 17.8 %collective-permute-start.16 = (bf16[64,2048]{1,0:T(8,128)(2,1)S(1)}, bf16[64,2048]{1,0:T(8,128)(2,1)}, u32[]{:S(2)}, u32[]{:S(2)}) collective-permute-start(bf16[64,2048]{1,0:T(8,128)(2,1)S(1)} %copy-done.21), channel_id=1, source_target_pairs={{0,4},{1,5},{2,6},{3,7},{4,0},{5,1},{6,2},{7,3},{8,12},{9,13},{10,... | collective-permute-start | bytes 786440 | tf_op jit(solution)/shard_map/ppermute | solution.py:236
  67.0 16.5 %collective-permute-start.15 = (bf16[64,2048]{1,0:T(8,128)(2,1)S(1)}, bf16[64,2048]{1,0:T(8,128)(2,1)}, u32[]{:S(2)}, u32[]{:S(2)}) collective-permute-start(bf16[64,2048]{1,0:T(8,128)(2,1)S(1)} %copy-done.21), channel_id=1, source_target_pairs={{0,2},{1,3},{2,0},{3,1},{4,6},{5,7},{6,4},{7,5},{8,10},{9,11},{10,... | collective-permute-start | bytes 786440 | tf_op jit(solution)/shard_map/ppermute | solution.py:236
  83.5 16.2 %copy-start.2 = (bf16[256,1792]{1,0:T(8,128)(2,1)}, bf16[256,1792]{1,0:T(8,128)(2,1)S(1)}, u32[]{:S(2)}) copy-start(bf16[256,1792]{1,0:T(8,128)(2,1)S(1)} %add_convert_fusion.2.refs_0_) | copy-start | bytes 2752516
  83.5 16.2 %collective-permute-start.19 = (bf16[256,1792]{1,0:T(8,128)(2,1)S(1)}, bf16[256,1792]{1,0:T(8,128)(2,1)S(1)}, u32[]{:S(2)}, u32[]{:S(2)}) collective-permute-start(bf16[256,1792]{1,0:T(8,128)(2,1)S(1)} %add_convert_fusion.1), channel_id=1, source_target_pairs={{8,16},{16,8},{9,17},{17,9},{10,18},{18,10},{11,19},{19,11},{12,20... | collective-permute-start | bytes 2752520 | tf_op jit(solution)/shard_map/ppermute | solution.py:291
  84.2 24.4 %collective-permute-start.18 = (bf16[256,1792]{1,0:T(8,128)(2,1)S(1)}, bf16[256,1792]{1,0:T(8,128)(2,1)S(1)}, u32[]{:S(2)}, u32[]{:S(2)}) collective-permute-start(bf16[256,1792]{1,0:T(8,128)(2,1)S(1)} %add_convert_fusion.2.refs_0_), channel_id=1, source_target_pairs={{8,0},{16,24},{9,1},{17,25},{10,2},{18,26},{11,3},{19,27},{12,4},{... | collective-permute-start | bytes 2752520 | tf_op jit(solution)/shard_map/ppermute | solution.py:297
  85.5 17.0 %collective-permute-start.20 = (bf16[64,2048]{1,0:T(8,128)(2,1)S(1)}, bf16[64,2048]{1,0:T(8,128)(2,1)}, u32[]{:S(2)}, u32[]{:S(2)}) collective-permute-start(bf16[64,2048]{1,0:T(8,128)(2,1)S(1)} %copy-done.21), channel_id=1, source_target_pairs={{0,1},{1,0},{2,3},{3,2},{4,5},{5,4},{6,7},{7,6},{8,9},{9,8},{10,11... | collective-permute-start | bytes 786440 | tf_op jit(solution)/shard_map/ppermute | solution.py:241
  85.6 16.9 %collective-permute-start.21 = (bf16[64,2048]{1,0:T(8,128)(2,1)}, bf16[64,2048]{1,0:T(8,128)(2,1)}, u32[]{:S(2)}, u32[]{:S(2)}) collective-permute-start(bf16[64,2048]{1,0:T(8,128)(2,1)} %collective-permute-done.15.refs_1_), channel_id=1, source_target_pairs={{0,1},{1,0},{2,3},{3,2},{4,5},{5,4},{6,7},{7,6},{8,9},{9,8},{10,11... | collective-permute-start | bytes 786440 | tf_op jit(solution)/shard_map/ppermute | solution.py:241
  86.1 16.4 %collective-permute-start.22 = (bf16[64,2048]{1,0:T(8,128)(2,1)}, bf16[64,2048]{1,0:T(8,128)(2,1)}, u32[]{:S(2)}, u32[]{:S(2)}) collective-permute-start(bf16[64,2048]{1,0:T(8,128)(2,1)} %collective-permute-done.16.refs_2_), channel_id=1, source_target_pairs={{0,1},{1,0},{2,3},{3,2},{4,5},{5,4},{6,7},{7,6},{8,9},{9,8},{10,11... | collective-permute-start | bytes 786440 | tf_op jit(solution)/shard_map/ppermute | solution.py:241
  100.7 1.9 %collective-permute-start.23 = (bf16[64,2048]{1,0:T(8,128)(2,1)}, bf16[64,2048]{1,0:T(8,128)(2,1)S(1)}, u32[]{:S(2)}, u32[]{:S(2)}) collective-permute-start(bf16[64,2048]{1,0:T(8,128)(2,1)} %collective-permute-done.17.refs_3_), channel_id=1, source_target_pairs={{0,1},{1,0},{2,3},{3,2},{4,5},{5,4},{6,7},{7,6},{8,9},{9,8},{10,11... | collective-permute-start | bytes 786440 | tf_op jit(solution)/shard_map/ppermute | solution.py:241
  108.6 25.2 %collective-permute-start.24 = (bf16[256,1792]{1,0:T(8,128)(2,1)S(1)}, bf16[256,1792]{1,0:T(8,128)(2,1)S(1)}, u32[]{:S(2)}, u32[]{:S(2)}) collective-permute-start(bf16[256,1792]{1,0:T(8,128)(2,1)S(1)} %add_convert_fusion.refs_0_), channel_id=1, source_target_pairs={{8,0},{16,24},{9,1},{17,25},{10,2},{18,26},{11,3},{19,27},{12,4},{... | collective-permute-start | bytes 2752520 | tf_op jit(solution)/shard_map/ppermute | solution.py:297
  133.8 11.7 %collective-permute-start.25 = (bf16[4,32,2048]{2,1,0:T(8,128)(2,1)}, bf16[4,32,2048]{2,1,0:T(8,128)(2,1)S(1)}, u32[]{:S(2)}, u32[]{:S(2)}) collective-permute-start(bf16[4,32,2048]{2,1,0:T(8,128)(2,1)} %get-tuple-element.169), channel_id=1, source_target_pairs={{0,1},{1,0},{2,3},{3,2},{4,5},{5,4},{6,7},{7,6},{8,9},{9,8},{10,11... | collective-permute-start | bytes 1572872 | tf_op jit(solution)/shard_map/ppermute | solution.py:302
  145.7 2.2 %collective-permute-start.26 = (bf16[4,32,2048]{2,1,0:T(8,128)(2,1)}, bf16[4,32,2048]{2,1,0:T(8,128)(2,1)S(1)}, u32[]{:S(2)}, u32[]{:S(2)}) collective-permute-start(bf16[4,32,2048]{2,1,0:T(8,128)(2,1)} %get-tuple-element.180), channel_id=1, source_target_pairs={{0,1},{1,0},{2,3},{3,2},{4,5},{5,4},{6,7},{7,6},{8,9},{9,8},{10,11... | collective-permute-start | bytes 1572872 | tf_op jit(solution)/shard_map/ppermute | solution.py:302
  148.1 17.1 %collective-permute-start.27 = (bf16[64,2048]{1,0:T(8,128)(2,1)S(1)}, bf16[64,2048]{1,0:T(8,128)(2,1)S(1)}, u32[]{:S(2)}, u32[]{:S(2)}) collective-permute-start(bf16[64,2048]{1,0:T(8,128)(2,1)S(1)} %pad_maximum_fusion.2), channel_id=1, source_target_pairs={{0,2},{1,3},{2,0},{3,1},{4,6},{5,7},{6,4},{7,5},{8,10},{9,11},{10,... | collective-permute-start | bytes 786440 | tf_op jit(solution)/shard_map/ppermute | solution.py:316
  149.7 15.6 %collective-permute-start.28 = (bf16[64,2048]{1,0:T(8,128)(2,1)S(1)}, bf16[64,2048]{1,0:T(8,128)(2,1)S(1)}, u32[]{:S(2)}, u32[]{:S(2)}) collective-permute-start(bf16[64,2048]{1,0:T(8,128)(2,1)S(1)} %pad_maximum_fusion.3), channel_id=1, source_target_pairs={{0,4},{1,5},{2,6},{3,7},{4,0},{5,1},{6,2},{7,3},{8,12},{9,13},{10,... | collective-permute-start | bytes 786440 | tf_op jit(solution)/shard_map/ppermute | solution.py:316
  150.5 14.8 %collective-permute-start.29 = (bf16[64,2048]{1,0:T(8,128)(2,1)S(1)}, bf16[64,2048]{1,0:T(8,128)(2,1)S(1)}, u32[]{:S(2)}, u32[]{:S(2)}) collective-permute-start(bf16[64,2048]{1,0:T(8,128)(2,1)S(1)} %pad_maximum_fusion.4), channel_id=1, source_target_pairs={{0,6},{1,7},{2,4},{3,5},{4,2},{5,3},{6,0},{7,1},{8,14},{9,15},{10,... | collective-permute-start | bytes 786440 | tf_op jit(solution)/shard_map/ppermute | solution.py:316
  (21 other events, 115.2 us)

commit v2 on v1

--- a/solution.py
+++ b/solution.py
@@ -34,9 +34,9 @@
     return 1.0 / (1.0 + jnp.exp(-gate))
 
 
-def hidden_grad_terms(q, pieces, others, axis, down):
+def hidden_grad_terms(pieces, others, axis, down):
     half = len(pieces)
-    _, rows, depth = pieces[0].shape
+    rows, depth = pieces[0].shape
     wide = down.shape[0]
     tokens = 2 * half * rows
     tile = tile_of(wide, 896)
@@ -57,7 +57,7 @@
     return pl.pallas_call(
         body,
         grid=(wide // tile,),
-        in_specs=[pl.BlockSpec((None, rows, depth), lambda i: (q, 0, 0))] * (2 * half)
+        in_specs=[pl.BlockSpec((rows, depth), lambda i: (0, 0))] * (2 * half)
         + [pl.BlockSpec((tile, depth), lambda i: (i, 0))],
         out_specs=[
             pl.BlockSpec((tokens, tile), lambda i: (0, i)),
@@ -336,15 +336,16 @@
         view = (row_tokens // block, CHUNKS, rows, wide)
         gates = gather_near(gate_saved.reshape(view), "row", n_row)
         up_saved = up_saved.reshape(view)
-        pieces = gather_parity(out_grad.reshape(CHUNKS, rows, depth), "col", n_col)
-        pieces, gates, up_saved, layer_input = hold(pieces, gates, up_saved, layer_input)
+        pieces = gather_parity(out_grad[:rows], "col", n_col)
+        pieces, gates, up_saved, out_grad, layer_input = hold(
+            pieces, gates, up_saved, out_grad, layer_input
+        )
         ups = gather_near(up_saved, "row", n_row)
         others = gather_others(pieces, "col", n_col)
-        first, grad = hidden_grad_terms(0, pieces, others, "col", down_weight)
+        first, grad = hidden_grad_terms(pieces, others, "col", down_weight)
         grads = [grad]
-        first, gates, ups, pieces, others, layer_input = hold(
-            first, gates, ups, pieces, others, layer_input
-        )
+        pieces = gather_parity(out_grad[rows:], "col", n_col)
+        first, gates, ups, pieces, layer_input = hold(first, gates, ups, pieces, layer_input)
 
         line = n_row == 4 and 2 * row_tokens * CHUNKS == tokens
         saved = [list(pair) for pair in zip(gates, ups)]
@@ -355,7 +356,8 @@
             saved += [[passed], [got.reshape(passed.shape)]]
         else:
             first = sum_in(first, "row", n_row)
-        second, grad = hidden_grad_terms(1, pieces, others, "col", down_weight)
+        others = gather_others(pieces, "col", n_col)
+        second, grad = hidden_grad_terms(pieces, others, "col", down_weight)
         grads.append(grad)
         first, second, saved, layer_input = hold(first, second, saved, layer_input)
 

time: 167 us -> 170 us (1.018)
  waiting for transfers between devices: 58.8 us -> 51.6 us
  starting transfers between devices: 32.1 us -> 37.2 us
  local copies, waits for them, and re-layouts: 3.55 us -> 8.3 us
    ppermute x6 -> x9, waiting for transfers between devices: 10.8 us -> 5.03 us  [gather_parity(): lax.ppermute(own, axis, [(i, i ^ 2 * k) for i in range(size)])]
    ppermute x6 -> x9, starting transfers between devices: 7.04 us -> 10.7 us  [gather_parity(): lax.ppermute(own, axis, [(i, i ^ 2 * k) for i in range(size)])]
    unnamed x46 -> x72, local copies, waits for them, and re-layouts: 3.46 us -> 6.38 us
    slice x0 -> x2, local copies, waits for them, and re-layouts: none -> 1.83 us  [the longest x1 0.91 us: shards(): pieces = gather_parity(out_grad[:rows], 'col', n_col)]
  transfers between devices with their start and end apart: 30 -> 37, of which waited for: 12 -> 12; matrix products, arithmetic and copies ran while one was open for 3% -> 4% of each run, Pallas kernels for 39% -> 38%
where the time goes in v2:
time: 170 us; the launch traced here: 169 us
  Pallas kernels  64.5 us (38%)
  waiting for transfers between devices  51.6 us (30%)
  starting transfers between devices  37.2 us (22%)
  local copies, waits for them, and re-layouts  8.3 us (5%)
  other arithmetic  5.91 us (3%)
    ppermute x2, waiting for transfers between devices, trade(): return lax.ppermute(given, axis, [(i, i ^ 1) for i in range(4)])  25.9 us
    pallas_call x2, Pallas kernels, input_grad_terms(): pl.pallas_call(body, grid=(depth // tile,), in_specs=[pl.BlockSpec((token...  21.7 us
    ppermute x2, waiting for transfers between devices, sum_out(): lax.ppermute(found[-1], axis, [(k + 1, k), (size - 2 - k, size - 1 - k)])  15.8 us
    pallas_call x1, Pallas kernels, down_weight_grads(): pl.pallas_call(body, grid=(wide // tile,), in_specs=[one if x.ndim == 4 e...  13.5 us
    pallas_call x1, Pallas kernels, projection_grads(): pl.pallas_call(body, grid=(depth // tile,), in_specs=[pl.BlockSpec((tile,...  13.4 us
    pallas_call x2, Pallas kernels, hidden_grad_terms(): pl.pallas_call(body, grid=(wide // tile,), in_specs=[pl.BlockSpec((rows,...  11.7 us
    ppermute x4, starting transfers between devices, gather_near(): return [shard] + [lax.ppermute(shard, axis, pairs) for pairs in swaps]  10.7 us
    ppermute x9, starting transfers between devices, gather_parity(): lax.ppermute(own, axis, [(i, i ^ 2 * k) for i in range(size)])  10.7 us
  transfers between devices with their start and end apart: 37, of which 12 were waited for; matrix products, arithmetic and copies ran while one was open for 4% of the time, Pallas kernels for 38%

profile of v2, /device:TPU:0, one launch (start us, length us, event | category | flops | bytes accessed | tf_op | source)
XLA Modules:
  0.0 168.7 jit_solution(9254725212435566253)
XLA Ops:
  1.3 5.9 %collective-permute-start.3 = (bf16[2,2,32,1792]{3,2,1,0:T(8,128)(2,1)}, bf16[2,2,32,1792]{3,2,1,0:T(8,128)(2,1)S(1)}, u32[]{:S(2)}, u32[]{:S(2)}) collective-permute-start(bf16[2,2,32,1792]{3,2,1,0:T(8,128)(2,1)} %bitcast.41), channel_id=1, source_target_pairs={{0,8},{8,0},{16,24},{24,16},{1,9},{9,1},{17,25},{25,17},{2,10},{10... | collective-permute-start | bytes 1376264 | tf_op jit(solution)/shard_map/ppermute | solution.py:267
  7.2 0.9 slice.6.refs_0_
  8.1 2.5 %collective-permute-start.2 = (bf16[32,2048]{1,0:T(8,128)(2,1)S(1)}, bf16[32,2048]{1,0:T(8,128)(2,1)S(1)}, u32[]{:S(2)}, u32[]{:S(2)}) collective-permute-start(bf16[32,2048]{1,0:T(8,128)(2,1)S(1)} %slice.6.refs_0_), channel_id=1, source_target_pairs={{0,6},{1,7},{2,4},{3,5},{4,2},{5,3},{6,0},{7,1},{8,14},{9,15},{10,... | collective-permute-start | bytes 393224 | tf_op jit(solution)/shard_map/ppermute | solution.py:236
  11.7 3.1 %collective-permute-done.2.refs_3_ = bf16[32,2048]{1,0:T(8,128)(2,1)S(1)} collective-permute-done((bf16[32,2048]{1,0:T(8,128)(2,1)S(1)}, bf16[32,2048]{1,0:T(8,128)(2,1)S(1)}, u32[]{:S(2)}, u32[]{:S(2)}) %collective-permute-start.2) | collective-permute-done | bytes 131104 | tf_op jit(solution)/shard_map/ppermute | solution.py:236
  14.8 1.8 %collective-permute-done.1.refs_2_ = bf16[32,2048]{1,0:T(8,128)(2,1)S(1)} collective-permute-done((bf16[32,2048]{1,0:T(8,128)(2,1)S(1)}, bf16[32,2048]{1,0:T(8,128)(2,1)S(1)}, u32[]{:S(2)}, u32[]{:S(2)}) %collective-permute-start.1) | collective-permute-done | bytes 131104 | tf_op jit(solution)/shard_map/ppermute | solution.py:236
  16.7 1.0 collective-permute-done.3.refs_2_
  18.4 3.5 %collective-permute-start.9 = (bf16[2,2,32,1792]{3,2,1,0:T(8,128)(2,1)}, bf16[2,2,32,1792]{3,2,1,0:T(8,128)(2,1)S(1)}, u32[]{:S(2)}, u32[]{:S(2)}) collective-permute-start(bf16[2,2,32,1792]{3,2,1,0:T(8,128)(2,1)} %bitcast.38), channel_id=1, source_target_pairs={{0,8},{8,0},{16,24},{24,16},{1,9},{9,1},{17,25},{25,17},{2,10},{10... | collective-permute-start | bytes 1376264 | tf_op jit(solution)/shard_map/ppermute | solution.py:267
  23.3 0.9 slice.7.refs_0_
  24.3 2.5 %collective-permute-start.13 = (bf16[32,2048]{1,0:T(8,128)(2,1)S(1)}, bf16[32,2048]{1,0:T(8,128)(2,1)S(1)}, u32[]{:S(2)}, u32[]{:S(2)}) collective-permute-start(bf16[32,2048]{1,0:T(8,128)(2,1)S(1)} %slice.7.refs_0_), channel_id=1, source_target_pairs={{0,6},{1,7},{2,4},{3,5},{4,2},{5,3},{6,0},{7,1},{8,14},{9,15},{10,... | collective-permute-start | bytes 393224 | tf_op jit(solution)/shard_map/ppermute | solution.py:236
  28.0 5.9 %hidden_grad_terms.2 = (bf16[256,1792]{1,0:T(8,128)(2,1)}, bf16[8,32,2048]{2,1,0:T(8,128)(2,1)}) custom-call(bf16[32,2048]{1,0:T(8,128)(2,1)} %copy-done.9, bf16[32,2048]{1,0:T(8,128)(2,1)} %copy-done.23, bf16[32,2048]{1,0:T(8,128)(2,1)} %copy-done.21, bf16[32,2048]{1,0:T(8,128)(2,1)} %copy-done.20, bf16[32,2048]{1,0:T(8,128)(2,1)} %copy-done.28, ...), custom_call_target="tpu_custom_call" | custom-call | flops 1879048192 | bytes 8388608 | tf_op jit(solution)/shard_map/hidden_grad_terms/pallas_call | solution.py:57
  36.5 1.1 pad_maximum_fusion.1
  41.8 5.9 %hidden_grad_terms.3 = (bf16[256,1792]{1,0:T(8,128)(2,1)}, bf16[8,32,2048]{2,1,0:T(8,128)(2,1)}) custom-call(bf16[32,2048]{1,0:T(8,128)(2,1)} %copy-done.10, bf16[32,2048]{1,0:T(8,128)(2,1)} %copy-done.26, bf16[32,2048]{1,0:T(8,128)(2,1)} %copy-done.24, bf16[32,2048]{1,0:T(8,128)(2,1)} %copy-done.22, bf16[32,2048]{1,0:T(8,128)(2,1)} %copy-done.32, ...), custom_call_target="tpu_custom_call" | custom-call | flops 1879048192 | bytes 8388608 | tf_op jit(solution)/shard_map/hidden_grad_terms/pallas_call | solution.py:57
  47.6 10.0 %collective-permute-done.14 = bf16[256,1792]{1,0:T(8,128)(2,1)} collective-permute-done((bf16[256,1792]{1,0:T(8,128)(2,1)S(1)}, bf16[256,1792]{1,0:T(8,128)(2,1)}, u32[]{:S(2)}, u32[]{:S(2)}) %collective-permute-start.14) | collective-permute-done | bytes 917536 | tf_op jit(solution)/shard_map/ppermute | solution.py:274
  57.6 1.4 add_convert_fusion.3
  59.2 4.6 %collective-permute-start.21 = (bf16[256,1792]{1,0:T(8,128)(2,1)S(1)}, bf16[256,1792]{1,0:T(8,128)(2,1)S(1)}, u32[]{:S(2)}, u32[]{:S(2)}) collective-permute-start(bf16[256,1792]{1,0:T(8,128)(2,1)S(1)} %bitcast_select_fusion), channel_id=1, source_target_pairs={{0,8},{8,0},{16,24},{24,16},{1,9},{9,1},{17,25},{25,17},{2,10},{10... | collective-permute-start | bytes 2752520 | tf_op jit(solution)/shard_map/ppermute | solution.py:274
  64.5 2.5 %collective-permute-start.24 = (bf16[64,2048]{1,0:T(8,128)(2,1)}, bf16[64,2048]{1,0:T(8,128)(2,1)S(1)}, u32[]{:S(2)}, u32[]{:S(2)}) collective-permute-start(bf16[64,2048]{1,0:T(8,128)(2,1)} %refs_0_), channel_id=1, source_target_pairs={{0,6},{1,7},{2,4},{3,5},{4,2},{5,3},{6,0},{7,1},{8,14},{9,15},{10,... | collective-permute-start | bytes 786440 | tf_op jit(solution)/shard_map/ppermute | solution.py:236
  68.1 15.9 %collective-permute-done.21 = bf16[256,1792]{1,0:T(8,128)(2,1)S(1)} collective-permute-done((bf16[256,1792]{1,0:T(8,128)(2,1)S(1)}, bf16[256,1792]{1,0:T(8,128)(2,1)S(1)}, u32[]{:S(2)}, u32[]{:S(2)}) %collective-permute-start.21) | collective-permute-done | bytes 917536 | tf_op jit(solution)/shard_map/ppermute | solution.py:274
  85.7 1.3 collective-permute-start.25
  87.7 13.5 %down_weight_grads.1 = (f32[1792,2048]{1,0:T(8,128)}, bf16[8,2,32,1792]{3,2,1,0:T(8,128)(2,1)}, bf16[8,2,32,1792]{3,2,1,0:T(8,128)(2,1)}) custom-call(bf16[2,2,32,1792]{3,2,1,0:T(8,128)(2,1)} %bitcast.42, bf16[2,2,32,1792]{3,2,1,0:T(8,128)(2,1)} %bitcast.39, bf16[2,2,32,1792]{3,2,1,0:T(8,128)(2,1)} %copy-done.14, bf16[2,2,32,1792]{3,2,1,0:T(8,128)(2,1)} %copy-done.17, ...), custom_call_target="tpu_custom_call" | custom-call | flops 3758096384 | bytes 14680064 | tf_op jit(solution)/shard_map/down_weight_grads/pallas_call | solution.py:115
  101.2 0.9 copy-done.7
  102.6 1.4 add_convert_fusion.refs_0_
  104.0 7.7 %collective-permute-done.25.refs_1_ = bf16[256,1792]{1,0:T(8,128)(2,1)S(1)} collective-permute-done((bf16[256,1792]{1,0:T(8,128)(2,1)S(1)}, bf16[256,1792]{1,0:T(8,128)(2,1)S(1)}, u32[]{:S(2)}, u32[]{:S(2)}) %collective-permute-start.25) | collective-permute-done | bytes 917536 | tf_op jit(solution)/shard_map/ppermute | solution.py:297
  111.8 1.5 collective-permute-start.31
  113.2 4.2 %turned.1.inputs_ref = bf16[2048,512]{1,0:T(8,128)(2,1)} custom-call(bf16[64,2048]{1,0:T(8,128)(2,1)} %refs_0_, bf16[64,2048]{1,0:T(8,128)(2,1)} %collective-permute-done.22.refs_1_, bf16[64,2048]{1,0:T(8,128)(2,1)} %collective-permute-done.23.refs_2_, bf16[64,2048]{1,0:T(8,128)(2,1)} %copy-done.18, bf16[64,2048]{1,0:T(8,128)(2,1)} %collective-permute-done.27.refs_4_, ...), custom_call_target="tpu_custom_call" | custom-call | flops 1 | bytes 4194304 | tf_op jit(solution)/shard_map/turned/pallas_call | solution.py:221
  117.5 10.9 %input_grad_terms.2 = (bf16[8,2,32,1792]{3,2,1,0:T(8,128)(2,1)}, bf16[8,2,32,1792]{3,2,1,0:T(8,128)(2,1)}, bf16[4,32,2048]{2,1,0:T(8,128)(2,1)}, bf16[4,32,2048]{2,1,0:T(8,128)(2,1)}) custom-call(bf16[256,1792]{1,0:T(8,128)(2,1)} %copy-done.2, bf16[256,1792]{1,0:T(8,128)(2,1)} %copy-done.6, bf16[8,2,32,1792]{3,2,1,0:T(8,128)(2,1)} %get-tuple-element.152.refs_2_, ...), custom_call_target="tpu_custom_call" | custom-call | flops 3758096384 | bytes 14680064 | tf_op jit(solution)/shard_map/input_grad_terms/pallas_call | solution.py:168
  128.3 8.1 %collective-permute-done.31.refs_1_ = bf16[256,1792]{1,0:T(8,128)(2,1)S(1)} collective-permute-done((bf16[256,1792]{1,0:T(8,128)(2,1)S(1)}, bf16[256,1792]{1,0:T(8,128)(2,1)S(1)}, u32[]{:S(2)}, u32[]{:S(2)}) %collective-permute-start.31) | collective-permute-done | bytes 917536 | tf_op jit(solution)/shard_map/ppermute | solution.py:297
  136.4 0.9 copy-done.8
  137.3 10.8 %input_grad_terms.3 = (bf16[8,2,32,1792]{3,2,1,0:T(8,128)(2,1)}, bf16[8,2,32,1792]{3,2,1,0:T(8,128)(2,1)}, bf16[4,32,2048]{2,1,0:T(8,128)(2,1)}, bf16[4,32,2048]{2,1,0:T(8,128)(2,1)}) custom-call(bf16[256,1792]{1,0:T(8,128)(2,1)} %copy-done.3, bf16[256,1792]{1,0:T(8,128)(2,1)} %copy-done.8, ...), custom_call_target="tpu_custom_call", output_to_operand_aliasing={{0}: (6, {}), {1}: (7, {})} | custom-call | flops 3758096384 | bytes 14680064 | tf_op jit(solution)/shard_map/input_grad_terms/pallas_call | solution.py:168
  148.5 2.0 %collective-permute-done.33 = bf16[4,32,2048]{2,1,0:T(8,128)(2,1)S(1)} collective-permute-done((bf16[4,32,2048]{2,1,0:T(8,128)(2,1)}, bf16[4,32,2048]{2,1,0:T(8,128)(2,1)S(1)}, u32[]{:S(2)}, u32[]{:S(2)}) %collective-permute-start.33) | collective-permute-done | bytes 524320 | tf_op jit(solution)/shard_map/ppermute | solution.py:302
  150.7 1.5 collective-permute-start.34
  152.3 1.6 collective-permute-start.35
  154.4 13.4 %projection_grads.1 = (f32[2048,1792]{1,0:T(8,128)}, f32[2048,1792]{1,0:T(8,128)}) custom-call(bf16[2048,512]{1,0:T(8,128)(2,1)} %turned.1.inputs_ref, bf16[512,1792]{1,0:T(8,128)(2,1)} %bitcast.30, bf16[512,1792]{1,0:T(8,128)(2,1)} %bitcast.31), custom_call_target="tpu_custom_call" | custom-call | flops 7516192768 | bytes 29360128 | tf_op jit(solution)/shard_map/projection_grads/pallas_call | solution.py:195
  (139 shorter events, 18.4 us)
Async XLA Ops:
  0.6 16.1 %collective-permute-start.4 = (bf16[2,2,32,1792]{3,2,1,0:T(8,128)(2,1)}, bf16[2,2,32,1792]{3,2,1,0:T(8,128)(2,1)S(1)}, u32[]{:S(2)}, u32[]{:S(2)}) collective-permute-start(bf16[2,2,32,1792]{3,2,1,0:T(8,128)(2,1)} %bitcast.40), channel_id=1, source_target_pairs={{8,16},{16,8},{9,17},{17,9},{10,18},{18,10},{11,19},{19,11},{12,20... | collective-permute-start | bytes 1376264 | tf_op jit(solution)/shard_map/ppermute | solution.py:267
  1.3 16.3 %collective-permute-start.3 = (bf16[2,2,32,1792]{3,2,1,0:T(8,128)(2,1)}, bf16[2,2,32,1792]{3,2,1,0:T(8,128)(2,1)S(1)}, u32[]{:S(2)}, u32[]{:S(2)}) collective-permute-start(bf16[2,2,32,1792]{3,2,1,0:T(8,128)(2,1)} %bitcast.41), channel_id=1, source_target_pairs={{0,8},{8,0},{16,24},{24,16},{1,9},{9,1},{17,25},{25,17},{2,10},{10... | collective-permute-start | bytes 1376264 | tf_op jit(solution)/shard_map/ppermute | solution.py:267
  8.1 6.6 %collective-permute-start.2 = (bf16[32,2048]{1,0:T(8,128)(2,1)S(1)}, bf16[32,2048]{1,0:T(8,128)(2,1)S(1)}, u32[]{:S(2)}, u32[]{:S(2)}) collective-permute-start(bf16[32,2048]{1,0:T(8,128)(2,1)S(1)} %slice.6.refs_0_), channel_id=1, source_target_pairs={{0,6},{1,7},{2,4},{3,5},{4,2},{5,3},{6,0},{7,1},{8,14},{9,15},{10,... | collective-permute-start | bytes 393224 | tf_op jit(solution)/shard_map/ppermute | solution.py:236
  10.7 5.9 %collective-permute-start.1 = (bf16[32,2048]{1,0:T(8,128)(2,1)S(1)}, bf16[32,2048]{1,0:T(8,128)(2,1)S(1)}, u32[]{:S(2)}, u32[]{:S(2)}) collective-permute-start(bf16[32,2048]{1,0:T(8,128)(2,1)S(1)} %slice.6.refs_0_), channel_id=1, source_target_pairs={{0,4},{1,5},{2,6},{3,7},{4,0},{5,1},{6,2},{7,3},{8,12},{9,13},{10,... | collective-permute-start | bytes 393224 | tf_op jit(solution)/shard_map/ppermute | solution.py:236
  11.2 5.5 %collective-permute-start = (bf16[32,2048]{1,0:T(8,128)(2,1)S(1)}, bf16[32,2048]{1,0:T(8,128)(2,1)S(1)}, u32[]{:S(2)}, u32[]{:S(2)}) collective-permute-start(bf16[32,2048]{1,0:T(8,128)(2,1)S(1)} %slice.6.refs_0_), channel_id=1, source_target_pairs={{0,2},{1,3},{2,0},{3,1},{4,6},{5,7},{6,4},{7,5},{8,10},{9,11},{10,... | collective-permute-start | bytes 393224 | tf_op jit(solution)/shard_map/ppermute | solution.py:236
  17.7 16.3 %collective-permute-start.10 = (bf16[2,2,32,1792]{3,2,1,0:T(8,128)(2,1)}, bf16[2,2,32,1792]{3,2,1,0:T(8,128)(2,1)S(1)}, u32[]{:S(2)}, u32[]{:S(2)}) collective-permute-start(bf16[2,2,32,1792]{3,2,1,0:T(8,128)(2,1)} %bitcast.37), channel_id=1, source_target_pairs={{8,16},{16,8},{9,17},{17,9},{10,18},{18,10},{11,19},{19,11},{12,20... | collective-permute-start | bytes 1376264 | tf_op jit(solution)/shard_map/ppermute | solution.py:267
  18.4 15.6 %collective-permute-start.9 = (bf16[2,2,32,1792]{3,2,1,0:T(8,128)(2,1)}, bf16[2,2,32,1792]{3,2,1,0:T(8,128)(2,1)S(1)}, u32[]{:S(2)}, u32[]{:S(2)}) collective-permute-start(bf16[2,2,32,1792]{3,2,1,0:T(8,128)(2,1)} %bitcast.38), channel_id=1, source_target_pairs={{0,8},{8,0},{16,24},{24,16},{1,9},{9,1},{17,25},{25,17},{2,10},{10... | collective-permute-start | bytes 1376264 | tf_op jit(solution)/shard_map/ppermute | solution.py:267
  21.8 2.4 %collective-permute-start.6 = (bf16[32,2048]{1,0:T(8,128)(2,1)S(1)}, bf16[32,2048]{1,0:T(8,128)(2,1)S(1)}, u32[]{:S(2)}, u32[]{:S(2)}) collective-permute-start(bf16[32,2048]{1,0:T(8,128)(2,1)S(1)} %collective-permute-done.refs_1_), channel_id=1, source_target_pairs={{0,1},{1,0},{2,3},{3,2},{4,5},{5,4},{6,7},{7,6},{8,9},{9,8},{10,11... | collective-permute-start | bytes 393224 | tf_op jit(solution)/shard_map/ppermute | solution.py:241
  22.3 4.5 %collective-permute-start.7 = (bf16[32,2048]{1,0:T(8,128)(2,1)S(1)}, bf16[32,2048]{1,0:T(8,128)(2,1)S(1)}, u32[]{:S(2)}, u32[]{:S(2)}) collective-permute-start(bf16[32,2048]{1,0:T(8,128)(2,1)S(1)} %collective-permute-done.1.refs_2_), channel_id=1, source_target_pairs={{0,1},{1,0},{2,3},{3,2},{4,5},{5,4},{6,7},{7,6},{8,9},{9,8},{10,11... | collective-permute-start | bytes 393224 | tf_op jit(solution)/shard_map/ppermute | solution.py:241
  23.2 4.1 %collective-permute-start.8 = (bf16[32,2048]{1,0:T(8,128)(2,1)S(1)}, bf16[32,2048]{1,0:T(8,128)(2,1)S(1)}, u32[]{:S(2)}, u32[]{:S(2)}) collective-permute-start(bf16[32,2048]{1,0:T(8,128)(2,1)S(1)} %collective-permute-done.2.refs_3_), channel_id=1, source_target_pairs={{0,1},{1,0},{2,3},{3,2},{4,5},{5,4},{6,7},{7,6},{8,9},{9,8},{10,11... | collective-permute-start | bytes 393224 | tf_op jit(solution)/shard_map/ppermute | solution.py:241
  24.3 9.6 %collective-permute-start.13 = (bf16[32,2048]{1,0:T(8,128)(2,1)S(1)}, bf16[32,2048]{1,0:T(8,128)(2,1)S(1)}, u32[]{:S(2)}, u32[]{:S(2)}) collective-permute-start(bf16[32,2048]{1,0:T(8,128)(2,1)S(1)} %slice.7.refs_0_), channel_id=1, source_target_pairs={{0,6},{1,7},{2,4},{3,5},{4,2},{5,3},{6,0},{7,1},{8,14},{9,15},{10,... | collective-permute-start | bytes 393224 | tf_op jit(solution)/shard_map/ppermute | solution.py:236
  26.8 7.0 %collective-permute-start.12 = (bf16[32,2048]{1,0:T(8,128)(2,1)S(1)}, bf16[32,2048]{1,0:T(8,128)(2,1)S(1)}, u32[]{:S(2)}, u32[]{:S(2)}) collective-permute-start(bf16[32,2048]{1,0:T(8,128)(2,1)S(1)} %slice.7.refs_0_), channel_id=1, source_target_pairs={{0,4},{1,5},{2,6},{3,7},{4,0},{5,1},{6,2},{7,3},{8,12},{9,13},{10,... | collective-permute-start | bytes 393224 | tf_op jit(solution)/shard_map/ppermute | solution.py:236
  27.3 6.6 %collective-permute-start.11 = (bf16[32,2048]{1,0:T(8,128)(2,1)S(1)}, bf16[32,2048]{1,0:T(8,128)(2,1)S(1)}, u32[]{:S(2)}, u32[]{:S(2)}) collective-permute-start(bf16[32,2048]{1,0:T(8,128)(2,1)S(1)} %slice.7.refs_0_), channel_id=1, source_target_pairs={{0,2},{1,3},{2,0},{3,1},{4,6},{5,7},{6,4},{7,5},{8,10},{9,11},{10,... | collective-permute-start | bytes 393224 | tf_op jit(solution)/shard_map/ppermute | solution.py:236
  35.6 22.0 %collective-permute-start.14 = (bf16[256,1792]{1,0:T(8,128)(2,1)S(1)}, bf16[256,1792]{1,0:T(8,128)(2,1)}, u32[]{:S(2)}, u32[]{:S(2)}) collective-permute-start(bf16[256,1792]{1,0:T(8,128)(2,1)S(1)} %bitcast_select_fusion.1), channel_id=1, source_target_pairs={{0,8},{8,0},{16,24},{24,16},{1,9},{9,1},{17,25},{25,17},{2,10},{10... | collective-permute-start | bytes 2752520 | tf_op jit(solution)/shard_map/ppermute | solution.py:274
  35.8 3.2 %collective-permute-start.15 = (bf16[32,2048]{1,0:T(8,128)(2,1)S(1)}, bf16[32,2048]{1,0:T(8,128)(2,1)S(1)}, u32[]{:S(2)}, u32[]{:S(2)}) collective-permute-start(bf16[32,2048]{1,0:T(8,128)(2,1)S(1)} %slice.7.refs_0_), channel_id=1, source_target_pairs={{0,1},{1,0},{2,3},{3,2},{4,5},{5,4},{6,7},{7,6},{8,9},{9,8},{10,11... | collective-permute-start | bytes 393224 | tf_op jit(solution)/shard_map/ppermute | solution.py:241
  37.6 21.4 %collective-permute-start.19 = (bf16[2,2,2,32,1792]{4,3,2,1,0:T(8,128)(2,1)S(1)}, bf16[2,2,2,32,1792]{4,3,2,1,0:T(8,128)(2,1)S(1)}, u32[]{:S(2)}, u32[]{:S(2)}) collective-permute-start(bf16[2,2,2,32,1792]{4,3,2,1,0:T(8,128)(2,1)S(1)} %pad_maximum_fusion.1), channel_id=1, source_target_pairs={{8,16},{16,8},{9,17},{17,9},{10,18},{18,10},{11,19},{19,11},{12,20... | collective-permute-start | bytes 2752520 | tf_op jit(solution)/shard_map/ppermute | solution.py:354
  59.2 24.8 %collective-permute-start.21 = (bf16[256,1792]{1,0:T(8,128)(2,1)S(1)}, bf16[256,1792]{1,0:T(8,128)(2,1)S(1)}, u32[]{:S(2)}, u32[]{:S(2)}) collective-permute-start(bf16[256,1792]{1,0:T(8,128)(2,1)S(1)} %bitcast_select_fusion), channel_id=1, source_target_pairs={{0,8},{8,0},{16,24},{24,16},{1,9},{9,1},{17,25},{25,17},{2,10},{10... | collective-permute-start | bytes 2752520 | tf_op jit(solution)/shard_map/ppermute | solution.py:274
  63.8 20.5 %collective-permute-start.20 = (bf16[256,1792]{1,0:T(8,128)(2,1)S(1)}, bf16[256,1792]{1,0:T(8,128)(2,1)S(1)}, u32[]{:S(2)}, u32[]{:S(2)}) collective-permute-start(bf16[256,1792]{1,0:T(8,128)(2,1)S(1)} %add_convert_fusion.3), channel_id=1, source_target_pairs={{8,16},{16,8},{9,17},{17,9},{10,18},{18,10},{11,19},{19,11},{12,20... | collective-permute-start | bytes 2752520 | tf_op jit(solution)/shard_map/ppermute | solution.py:291
  64.5 20.4 %collective-permute-start.24 = (bf16[64,2048]{1,0:T(8,128)(2,1)}, bf16[64,2048]{1,0:T(8,128)(2,1)S(1)}, u32[]{:S(2)}, u32[]{:S(2)}) collective-permute-start(bf16[64,2048]{1,0:T(8,128)(2,1)} %refs_0_), channel_id=1, source_target_pairs={{0,6},{1,7},{2,4},{3,5},{4,2},{5,3},{6,0},{7,1},{8,14},{9,15},{10,... | collective-permute-start | bytes 786440 | tf_op jit(solution)/shard_map/ppermute | solution.py:236
  67.0 18.0 %collective-permute-start.23 = (bf16[64,2048]{1,0:T(8,128)(2,1)}, bf16[64,2048]{1,0:T(8,128)(2,1)}, u32[]{:S(2)}, u32[]{:S(2)}) collective-permute-start(bf16[64,2048]{1,0:T(8,128)(2,1)} %refs_0_), channel_id=1, source_target_pairs={{0,4},{1,5},{2,6},{3,7},{4,0},{5,1},{6,2},{7,3},{8,12},{9,13},{10,... | collective-permute-start | bytes 786440 | tf_op jit(solution)/shard_map/ppermute | solution.py:236
  67.5 17.5 %collective-permute-start.22 = (bf16[64,2048]{1,0:T(8,128)(2,1)}, bf16[64,2048]{1,0:T(8,128)(2,1)}, u32[]{:S(2)}, u32[]{:S(2)}) collective-permute-start(bf16[64,2048]{1,0:T(8,128)(2,1)} %refs_0_), channel_id=1, source_target_pairs={{0,2},{1,3},{2,0},{3,1},{4,6},{5,7},{6,4},{7,5},{8,10},{9,11},{10,... | collective-permute-start | bytes 786440 | tf_op jit(solution)/shard_map/ppermute | solution.py:236
  85.0 16.2 %collective-permute-start.26 = (bf16[256,1792]{1,0:T(8,128)(2,1)S(1)}, bf16[256,1792]{1,0:T(8,128)(2,1)S(1)}, u32[]{:S(2)}, u32[]{:S(2)}) collective-permute-start(bf16[256,1792]{1,0:T(8,128)(2,1)S(1)} %add_convert_fusion.1), channel_id=1, source_target_pairs={{8,16},{16,8},{9,17},{17,9},{10,18},{18,10},{11,19},{19,11},{12,20... | collective-permute-start | bytes 2752520 | tf_op jit(solution)/shard_map/ppermute | solution.py:291
  85.7 26.1 %collective-permute-start.25 = (bf16[256,1792]{1,0:T(8,128)(2,1)S(1)}, bf16[256,1792]{1,0:T(8,128)(2,1)S(1)}, u32[]{:S(2)}, u32[]{:S(2)}) collective-permute-start(bf16[256,1792]{1,0:T(8,128)(2,1)S(1)} %add_convert_fusion.2.refs_0_), channel_id=1, source_target_pairs={{8,0},{16,24},{9,1},{17,25},{10,2},{18,26},{11,3},{19,27},{12,4},{... | collective-permute-start | bytes 2752520 | tf_op jit(solution)/shard_map/ppermute | solution.py:297
  87.0 17.0 %collective-permute-start.27 = (bf16[64,2048]{1,0:T(8,128)(2,1)}, bf16[64,2048]{1,0:T(8,128)(2,1)}, u32[]{:S(2)}, u32[]{:S(2)}) collective-permute-start(bf16[64,2048]{1,0:T(8,128)(2,1)} %refs_0_), channel_id=1, source_target_pairs={{0,1},{1,0},{2,3},{3,2},{4,5},{5,4},{6,7},{7,6},{8,9},{9,8},{10,11... | collective-permute-start | bytes 786440 | tf_op jit(solution)/shard_map/ppermute | solution.py:241
  87.1 16.9 %collective-permute-start.28 = (bf16[64,2048]{1,0:T(8,128)(2,1)}, bf16[64,2048]{1,0:T(8,128)(2,1)}, u32[]{:S(2)}, u32[]{:S(2)}) collective-permute-start(bf16[64,2048]{1,0:T(8,128)(2,1)} %collective-permute-done.22.refs_1_), channel_id=1, source_target_pairs={{0,1},{1,0},{2,3},{3,2},{4,5},{5,4},{6,7},{7,6},{8,9},{9,8},{10,11... | collective-permute-start | bytes 786440 | tf_op jit(solution)/shard_map/ppermute | solution.py:241
  87.6 16.4 %collective-permute-start.29 = (bf16[64,2048]{1,0:T(8,128)(2,1)}, bf16[64,2048]{1,0:T(8,128)(2,1)}, u32[]{:S(2)}, u32[]{:S(2)}) collective-permute-start(bf16[64,2048]{1,0:T(8,128)(2,1)} %collective-permute-done.23.refs_2_), channel_id=1, source_target_pairs={{0,1},{1,0},{2,3},{3,2},{4,5},{5,4},{6,7},{7,6},{8,9},{9,8},{10,11... | collective-permute-start | bytes 786440 | tf_op jit(solution)/shard_map/ppermute | solution.py:241
  111.8 24.6 %collective-permute-start.31 = (bf16[256,1792]{1,0:T(8,128)(2,1)S(1)}, bf16[256,1792]{1,0:T(8,128)(2,1)S(1)}, u32[]{:S(2)}, u32[]{:S(2)}) collective-permute-start(bf16[256,1792]{1,0:T(8,128)(2,1)S(1)} %add_convert_fusion.refs_0_), channel_id=1, source_target_pairs={{8,0},{16,24},{9,1},{17,25},{10,2},{18,26},{11,3},{19,27},{12,4},{... | collective-permute-start | bytes 2752520 | tf_op jit(solution)/shard_map/ppermute | solution.py:297
  136.4 11.8 %collective-permute-start.32 = (bf16[4,32,2048]{2,1,0:T(8,128)(2,1)}, bf16[4,32,2048]{2,1,0:T(8,128)(2,1)S(1)}, u32[]{:S(2)}, u32[]{:S(2)}) collective-permute-start(bf16[4,32,2048]{2,1,0:T(8,128)(2,1)} %get-tuple-element.163), channel_id=1, source_target_pairs={{0,1},{1,0},{2,3},{3,2},{4,5},{5,4},{6,7},{7,6},{8,9},{9,8},{10,11... | collective-permute-start | bytes 1572872 | tf_op jit(solution)/shard_map/ppermute | solution.py:302
  148.3 2.2 %collective-permute-start.33 = (bf16[4,32,2048]{2,1,0:T(8,128)(2,1)}, bf16[4,32,2048]{2,1,0:T(8,128)(2,1)S(1)}, u32[]{:S(2)}, u32[]{:S(2)}) collective-permute-start(bf16[4,32,2048]{2,1,0:T(8,128)(2,1)} %get-tuple-element.174), channel_id=1, source_target_pairs={{0,1},{1,0},{2,3},{3,2},{4,5},{5,4},{6,7},{7,6},{8,9},{9,8},{10,11... | collective-permute-start | bytes 1572872 | tf_op jit(solution)/shard_map/ppermute | solution.py:302
  150.7 17.2 %collective-permute-start.34 = (bf16[64,2048]{1,0:T(8,128)(2,1)S(1)}, bf16[64,2048]{1,0:T(8,128)(2,1)S(1)}, u32[]{:S(2)}, u32[]{:S(2)}) collective-permute-start(bf16[64,2048]{1,0:T(8,128)(2,1)S(1)} %pad_maximum_fusion.2), channel_id=1, source_target_pairs={{0,2},{1,3},{2,0},{3,1},{4,6},{5,7},{6,4},{7,5},{8,10},{9,11},{10,... | collective-permute-start | bytes 786440 | tf_op jit(solution)/shard_map/ppermute | solution.py:316
  152.3 15.6 %collective-permute-start.35 = (bf16[64,2048]{1,0:T(8,128)(2,1)S(1)}, bf16[64,2048]{1,0:T(8,128)(2,1)S(1)}, u32[]{:S(2)}, u32[]{:S(2)}) collective-permute-start(bf16[64,2048]{1,0:T(8,128)(2,1)S(1)} %pad_maximum_fusion.3), channel_id=1, source_target_pairs={{0,4},{1,5},{2,6},{3,7},{4,0},{5,1},{6,2},{7,3},{8,12},{9,13},{10,... | collective-permute-start | bytes 786440 | tf_op jit(solution)/shard_map/ppermute | solution.py:316
  153.9 14.0 %collective-permute-start.36 = (bf16[64,2048]{1,0:T(8,128)(2,1)S(1)}, bf16[64,2048]{1,0:T(8,128)(2,1)S(1)}, u32[]{:S(2)}, u32[]{:S(2)}) collective-permute-start(bf16[64,2048]{1,0:T(8,128)(2,1)S(1)} %pad_maximum_fusion.4), channel_id=1, source_target_pairs={{0,6},{1,7},{2,4},{3,5},{4,2},{5,3},{6,0},{7,1},{8,14},{9,15},{10,... | collective-permute-start | bytes 786440 | tf_op jit(solution)/shard_map/ppermute | solution.py:316
  (41 other events, 254.7 us)

commit v3 on v1

--- a/solution.py
+++ b/solution.py
@@ -132,48 +132,87 @@
     tokens = cols * rows
     levels = len(sums)
     tile = tile_of(depth, 512)
+    steps = depth // tile
 
     def body(*refs):
-        sums_refs, refs = refs[:levels], refs[levels:]
-        by_gate_ref, by_up_ref, gate_w_ref, up_w_ref = refs[:4]
-        gate_out, up_out, keep_ref, send_ref = refs[-4:]
-
-        @pl.when(pl.program_id(0) == 0)
-        def _():
-            here = lax.axis_index(axes[0])
-            hidden_grad = sums_refs[0][...].astype(jnp.float32)
-            for level in range(1, levels):
-                at_level = (here == levels - 1 - level) | (here == levels + level)
-                other = sums_refs[level][...].astype(jnp.float32)
-                hidden_grad = jnp.where(at_level, other, hidden_grad)
-            for by_ref, out in ((by_gate_ref, gate_out), (by_up_ref, up_out)):
-                by = by_ref[...].reshape(tokens, wide).astype(jnp.float32)
-                out[...] = (hidden_grad * by).astype(jnp.bfloat16).reshape(cols, rows, wide)
+        sums_refs, by_refs, weight_refs = refs[:levels], refs[levels : levels + 2], refs[levels + 2 :][:2]
+        outs, keep_ref, send_ref = refs[-11:-9], refs[-9], refs[-8]
+        sums_in, by_in, weights_in, grads, first_sems, weight_sems, out_sems = refs[-7:]
+
+        def weight_copy(k, i):
+            part = pl.ds(pl.multiple_of(i * tile, tile), tile)
+            return pltpu.make_async_copy(
+                weight_refs[k].at[part], weights_in.at[k, part], weight_sems.at[k, i]
+            )
+
+        firsts = [
+            pltpu.make_async_copy(sums_refs[k], sums_in.at[k], first_sems.at[k]) for k in range(levels)
+        ]
+        firsts += [
+            pltpu.make_async_copy(by_refs[k].at[:, q], by_in.at[k], first_sems.at[levels + k])
+            for k in range(2)
+        ]
+        for copy in firsts:
+            copy.start()
+        for i in range(steps):
+            for k in range(2):
+                weight_copy(k, i).start()
+        for copy in firsts:
+            copy.wait()
+
+        here = lax.axis_index(axes[0])
+        hidden_grad = sums_in[0].astype(jnp.float32)
+        for level in range(1, levels):
+            at_level = (here == levels - 1 - level) | (here == levels + level)
+            hidden_grad = jnp.where(at_level, sums_in[level].astype(jnp.float32), hidden_grad)
+        for k in range(2):
+            by = by_in[k].reshape(tokens, wide).astype(jnp.float32)
+            grads[k] = (hidden_grad * by).astype(jnp.bfloat16).reshape(cols, rows, wide)
+        out_copies = [
+            pltpu.make_async_copy(grads.at[k], outs[k].at[:, q], out_sems.at[k]) for k in range(2)
+        ]
+        for copy in out_copies:
+            copy.start()
 
         odd = lax.axis_index(axes[1]) % 2 == 1
-        gate_grad = gate_out[...].reshape(tokens, wide)
-        up_grad = up_out[...].reshape(tokens, wide)
-        for part in halves_of(tile):
-            res = dot(gate_grad, gate_w_ref[part], ((1,), (1,)))
-            res += dot(up_grad, up_w_ref[part], ((1,), (1,)))
-            res = res.astype(jnp.bfloat16).reshape(cols // 2, 2, rows, part.stop - part.start)
-            keep_ref[:, :, part] = jnp.where(odd, res[:, 1], res[:, 0])
-            send_ref[:, :, part] = jnp.where(odd, res[:, 0], res[:, 1])
-
-    into = pl.BlockSpec((cols, None, rows, wide), lambda i: (0, q, 0, 0))
-    weight = pl.BlockSpec((tile, wide), lambda i: (i, 0))
-    half = pl.BlockSpec((cols // 2, rows, tile), lambda i: (0, 0, i))
+        gate_grad = grads[0].reshape(tokens, wide)
+        up_grad = grads[1].reshape(tokens, wide)
+
+        @pl.loop(0, steps)
+        def _(i):
+            for k in range(2):
+                weight_copy(k, i).wait()
+            for part in halves_of(tile):
+                size = part.stop - part.start
+                at = pl.ds(pl.multiple_of(i * tile + part.start, 128), size)
+                res = dot(gate_grad, weights_in[0, at], ((1,), (1,)))
+                res += dot(up_grad, weights_in[1, at], ((1,), (1,)))
+                res = res.astype(jnp.bfloat16).reshape(cols // 2, 2, rows, size)
+                keep_ref[:, :, at] = jnp.where(odd, res[:, 1], res[:, 0])
+                send_ref[:, :, at] = jnp.where(odd, res[:, 0], res[:, 1])
+
+        for copy in out_copies:
+            copy.wait()
+
+    anywhere = pl.BlockSpec(memory_space=pl.ANY)
+    in_vmem = pl.BlockSpec(memory_space=pltpu.VMEM)
     halves = jax.ShapeDtypeStruct((cols // 2, rows, depth), jnp.bfloat16)
     whole = jax.ShapeDtypeStruct((cols, chunks, rows, wide), jnp.bfloat16)
     return pl.pallas_call(
         body,
-        grid=(depth // tile,),
-        in_specs=[pl.BlockSpec((tokens, wide), lambda i: (0, 0))] * levels
-        + [into, into, weight, weight]
-        + [pl.BlockSpec(memory_space=pl.ANY)] * len(made),
-        out_specs=[into, into, half, half],
+        in_specs=[anywhere] * (levels + 4 + len(made)),
+        out_specs=[anywhere, anywhere, in_vmem, in_vmem],
         out_shape=[whole, whole, halves, halves],
         input_output_aliases={levels + 4 + j: j for j in range(len(made))},
+        scratch_shapes=[
+            pltpu.VMEM((levels, tokens, wide), jnp.bfloat16),
+            pltpu.VMEM((2, cols, rows, wide), jnp.bfloat16),
+            pltpu.VMEM((2, depth, wide), jnp.bfloat16),
+            pltpu.VMEM((2, cols, rows, wide), jnp.bfloat16),
+            pltpu.SemaphoreType.DMA((levels + 2,)),
+            pltpu.SemaphoreType.DMA((2, steps)),
+            pltpu.SemaphoreType.DMA((2,)),
+        ],
         compiler_params=params(),
         cost_estimate=cost(4 * tokens * wide * depth, 4 * wide * depth),
         name="input_grad_terms",

time: 167 us -> 169 us (1.012)
  Pallas kernels: 64.6 us -> 68.6 us
  waiting for transfers between devices: 58.8 us -> 56.8 us
    pallas_call x2, Pallas kernels: 21.7 us -> 25.7 us  [input_grad_terms(): pl.pallas_call(body, in_specs=[anywhere] * (levels + 4 + len(made)), out_...]
    ppermute x2, waiting for transfers between devices: 14.7 us -> 12.7 us  [sum_out(): lax.ppermute(found[-1], axis, [(k + 1, k), (size - 2 - k, size - 1 - k)])]
  transfers between devices with their start and end apart: 30 -> 30, of which waited for: 12 -> 12; matrix products, arithmetic and copies ran while one was open for 3% -> 3% of each run, Pallas kernels for 39% -> 41%
where the time goes in v3:
time: 169 us; the launch traced here: 168 us
  Pallas kernels  68.6 us (41%)
  waiting for transfers between devices  56.8 us (34%)
  starting transfers between devices  32.1 us (19%)
  other arithmetic  6.01 us (4%)
  local copies, waits for them, and re-layouts  3.55 us (2%)
    ppermute x2, waiting for transfers between devices, trade(): return lax.ppermute(given, axis, [(i, i ^ 1) for i in range(4)])  27.5 us
    pallas_call x2, Pallas kernels, input_grad_terms(): pl.pallas_call(body, in_specs=[anywhere] * (levels + 4 + len(made)), out_...  25.7 us
    pallas_call x1, Pallas kernels, down_weight_grads(): pl.pallas_call(body, grid=(wide // tile,), in_specs=[one if x.ndim == 4 e...  13.5 us
    pallas_call x1, Pallas kernels, projection_grads(): pl.pallas_call(body, grid=(depth // tile,), in_specs=[pl.BlockSpec((tile,...  13.4 us
    ppermute x2, waiting for transfers between devices, sum_out(): lax.ppermute(found[-1], axis, [(k + 1, k), (size - 2 - k, size - 1 - k)])  12.7 us
    pallas_call x2, Pallas kernels, hidden_grad_terms(): pl.pallas_call(body, grid=(wide // tile,), in_specs=[pl.BlockSpec((None,...  11.7 us
    ppermute x6, waiting for transfers between devices, gather_parity(): lax.ppermute(own, axis, [(i, i ^ 2 * k) for i in range(size)])  10.8 us
    ppermute x4, starting transfers between devices, gather_near(): return [shard] + [lax.ppermute(shard, axis, pairs) for pairs in swaps]  9.36 us
  transfers between devices with their start and end apart: 30, of which 12 were waited for; matrix products, arithmetic and copies ran while one was open for 3% of the time, Pallas kernels for 41%

profile of v3, /device:TPU:0, one launch (start us, length us, event | category | flops | bytes accessed | tf_op | source)
XLA Modules:
  0.0 168.2 jit_solution(208311116505578128)
XLA Ops:
  1.3 5.9 %collective-permute-start.3 = (bf16[2,2,32,1792]{3,2,1,0:T(8,128)(2,1)}, bf16[2,2,32,1792]{3,2,1,0:T(8,128)(2,1)S(1)}, u32[]{:S(2)}, u32[]{:S(2)}) collective-permute-start(bf16[2,2,32,1792]{3,2,1,0:T(8,128)(2,1)} %bitcast.47), channel_id=1, source_target_pairs={{0,8},{8,0},{16,24},{24,16},{1,9},{9,1},{17,25},{25,17},{2,10},{10... | collective-permute-start | bytes 1376264 | tf_op jit(solution)/shard_map/ppermute | solution.py:306
  7.2 2.4 %collective-permute-start.2 = (bf16[2,32,2048]{2,1,0:T(8,128)(2,1)}, bf16[2,32,2048]{2,1,0:T(8,128)(2,1)S(1)}, u32[]{:S(2)}, u32[]{:S(2)}) collective-permute-start(bf16[2,32,2048]{2,1,0:T(8,128)(2,1)} %bitcast.33), channel_id=1, source_target_pairs={{0,6},{1,7},{2,4},{3,5},{4,2},{5,3},{6,0},{7,1},{8,14},{9,15},{10,... | collective-permute-start | bytes 786440 | tf_op jit(solution)/shard_map/ppermute | solution.py:275
  10.7 6.9 %collective-permute-done.2.refs_3_ = bf16[2,32,2048]{2,1,0:T(8,128)(2,1)S(1)} collective-permute-done((bf16[2,32,2048]{2,1,0:T(8,128)(2,1)}, bf16[2,32,2048]{2,1,0:T(8,128)(2,1)S(1)}, u32[]{:S(2)}, u32[]{:S(2)}) %collective-permute-start.2) | collective-permute-done | bytes 262176 | tf_op jit(solution)/shard_map/ppermute | solution.py:275
  17.6 3.8 %collective-permute-done.1.refs_2_ = bf16[2,32,2048]{2,1,0:T(8,128)(2,1)S(1)} collective-permute-done((bf16[2,32,2048]{2,1,0:T(8,128)(2,1)}, bf16[2,32,2048]{2,1,0:T(8,128)(2,1)S(1)}, u32[]{:S(2)}, u32[]{:S(2)}) %collective-permute-start.1) | collective-permute-done | bytes 262176 | tf_op jit(solution)/shard_map/ppermute | solution.py:275
  22.3 2.1 %collective-permute-start.9 = (bf16[2,2,32,1792]{3,2,1,0:T(8,128)(2,1)}, bf16[2,2,32,1792]{3,2,1,0:T(8,128)(2,1)}, u32[]{:S(2)}, u32[]{:S(2)}) collective-permute-start(bf16[2,2,32,1792]{3,2,1,0:T(8,128)(2,1)} %bitcast.44), channel_id=1, source_target_pairs={{0,8},{8,0},{16,24},{24,16},{1,9},{9,1},{17,25},{25,17},{2,10},{10... | collective-permute-start | bytes 1376264 | tf_op jit(solution)/shard_map/ppermute | solution.py:306
  25.0 0.9 collective-permute-done.6.refs_5_
  27.7 5.9 %hidden_grad_terms.2 = (bf16[256,1792]{1,0:T(8,128)(2,1)}, bf16[8,32,2048]{2,1,0:T(8,128)(2,1)}) custom-call(bf16[2,32,2048]{2,1,0:T(8,128)(2,1)} %bitcast.37, bf16[2,32,2048]{2,1,0:T(8,128)(2,1)} %copy-done.6, bf16[2,32,2048]{2,1,0:T(8,128)(2,1)} %copy-done.5, bf16[2,32,2048]{2,1,0:T(8,128)(2,1)} %copy-done.4, bf16[2,32,2048]{2,1,0:T(8,128)(2,1)} %copy-done.7, ...), custom_call_target="tpu_custom_call" | custom-call | flops 1879048192 | bytes 8388608 | tf_op jit(solution)/shard_map/hidden_grad_terms/pallas_call | solution.py:57
  33.6 2.0 %collective-permute-done.9.refs_3_ = bf16[2,2,32,1792]{3,2,1,0:T(8,128)(2,1)} collective-permute-done((bf16[2,2,32,1792]{3,2,1,0:T(8,128)(2,1)}, bf16[2,2,32,1792]{3,2,1,0:T(8,128)(2,1)}, u32[]{:S(2)}, u32[]{:S(2)}) %collective-permute-start.9) | collective-permute-done | bytes 458784 | tf_op jit(solution)/shard_map/ppermute | solution.py:306
  35.9 1.9 %collective-permute-start.11 = (bf16[256,1792]{1,0:T(8,128)(2,1)S(1)}, bf16[256,1792]{1,0:T(8,128)(2,1)}, u32[]{:S(2)}, u32[]{:S(2)}) collective-permute-start(bf16[256,1792]{1,0:T(8,128)(2,1)S(1)} %bitcast_select_fusion.1), channel_id=1, source_target_pairs={{0,8},{8,0},{16,24},{24,16},{1,9},{9,1},{17,25},{25,17},{2,10},{10... | collective-permute-start | bytes 2752520 | tf_op jit(solution)/shard_map/ppermute | solution.py:313
  37.8 1.2 pad_maximum_fusion.1
  39.8 5.9 %hidden_grad_terms.3 = (bf16[256,1792]{1,0:T(8,128)(2,1)}, bf16[8,32,2048]{2,1,0:T(8,128)(2,1)}) custom-call(bf16[2,32,2048]{2,1,0:T(8,128)(2,1)} %bitcast.38, bf16[2,32,2048]{2,1,0:T(8,128)(2,1)} %copy-done.6, bf16[2,32,2048]{2,1,0:T(8,128)(2,1)} %copy-done.5, bf16[2,32,2048]{2,1,0:T(8,128)(2,1)} %copy-done.4, bf16[2,32,2048]{2,1,0:T(8,128)(2,1)} %copy-done.7, ...), custom_call_target="tpu_custom_call" | custom-call | flops 1879048192 | bytes 8388608 | tf_op jit(solution)/shard_map/hidden_grad_terms/pallas_call | solution.py:57
  45.7 12.6 %collective-permute-done.11 = bf16[256,1792]{1,0:T(8,128)(2,1)} collective-permute-done((bf16[256,1792]{1,0:T(8,128)(2,1)S(1)}, bf16[256,1792]{1,0:T(8,128)(2,1)}, u32[]{:S(2)}, u32[]{:S(2)}) %collective-permute-start.11) | collective-permute-done | bytes 917536 | tf_op jit(solution)/shard_map/ppermute | solution.py:313
  58.3 1.4 add_convert_fusion.3
  59.9 3.4 %collective-permute-start.14 = (bf16[256,1792]{1,0:T(8,128)(2,1)S(1)}, bf16[256,1792]{1,0:T(8,128)(2,1)S(1)}, u32[]{:S(2)}, u32[]{:S(2)}) collective-permute-start(bf16[256,1792]{1,0:T(8,128)(2,1)S(1)} %bitcast_select_fusion), channel_id=1, source_target_pairs={{0,8},{8,0},{16,24},{24,16},{1,9},{9,1},{17,25},{25,17},{2,10},{10... | collective-permute-start | bytes 2752520 | tf_op jit(solution)/shard_map/ppermute | solution.py:313
  64.0 1.7 %collective-permute-start.17 = (bf16[64,2048]{1,0:T(8,128)(2,1)S(1)}, bf16[64,2048]{1,0:T(8,128)(2,1)}, u32[]{:S(2)}, u32[]{:S(2)}) collective-permute-start(bf16[64,2048]{1,0:T(8,128)(2,1)S(1)} %copy-done.21), channel_id=1, source_target_pairs={{0,6},{1,7},{2,4},{3,5},{4,2},{5,3},{6,0},{7,1},{8,14},{9,15},{10,... | collective-permute-start | bytes 786440 | tf_op jit(solution)/shard_map/ppermute | solution.py:275
  65.7 1.3 collective-permute-start.16
  67.5 14.9 %collective-permute-done.14 = bf16[256,1792]{1,0:T(8,128)(2,1)S(1)} collective-permute-done((bf16[256,1792]{1,0:T(8,128)(2,1)S(1)}, bf16[256,1792]{1,0:T(8,128)(2,1)S(1)}, u32[]{:S(2)}, u32[]{:S(2)}) %collective-permute-start.14) | collective-permute-done | bytes 917536 | tf_op jit(solution)/shard_map/ppermute | solution.py:313
  84.2 1.3 collective-permute-start.18
  86.2 13.5 %down_weight_grads.1 = (f32[1792,2048]{1,0:T(8,128)}, bf16[8,2,32,1792]{3,2,1,0:T(8,128)(2,1)}, bf16[8,2,32,1792]{3,2,1,0:T(8,128)(2,1)}) custom-call(bf16[2,2,32,1792]{3,2,1,0:T(8,128)(2,1)} %bitcast.48, bf16[2,2,32,1792]{3,2,1,0:T(8,128)(2,1)} %bitcast.45, bf16[2,2,32,1792]{3,2,1,0:T(8,128)(2,1)} %copy-done.19, ...), custom_call_target="tpu_custom_call" | custom-call | flops 3758096384 | bytes 14680064 | tf_op jit(solution)/shard_map/down_weight_grads/pallas_call | solution.py:115
  99.7 0.9 copy-done.14
  101.1 1.4 add_convert_fusion.refs_0_
  102.6 6.0 %collective-permute-done.18.refs_1_ = bf16[256,1792]{1,0:T(8,128)(2,1)S(1)} collective-permute-done((bf16[256,1792]{1,0:T(8,128)(2,1)S(1)}, bf16[256,1792]{1,0:T(8,128)(2,1)S(1)}, u32[]{:S(2)}, u32[]{:S(2)}) %collective-permute-start.18) | collective-permute-done | bytes 917536 | tf_op jit(solution)/shard_map/ppermute | solution.py:336
  108.6 1.5 collective-permute-start.24
  110.1 4.2 %turned.1.inputs_ref = bf16[2048,512]{1,0:T(8,128)(2,1)} custom-call(bf16[64,2048]{1,0:T(8,128)(2,1)} %refs_0_, bf16[64,2048]{1,0:T(8,128)(2,1)} %collective-permute-done.15.refs_1_, bf16[64,2048]{1,0:T(8,128)(2,1)} %collective-permute-done.16.refs_2_, bf16[64,2048]{1,0:T(8,128)(2,1)} %collective-permute-done.17.refs_3_, ...), custom_call_target="tpu_custom_call" | custom-call | flops 1 | bytes 4194304 | tf_op jit(solution)/shard_map/turned/pallas_call | solution.py:260
  114.3 12.8 %input_grad_terms.2 = (bf16[8,2,32,1792]{3,2,1,0:T(8,128)(2,1)}, bf16[8,2,32,1792]{3,2,1,0:T(8,128)(2,1)}, bf16[4,32,2048]{2,1,0:T(8,128)(2,1)}, bf16[4,32,2048]{2,1,0:T(8,128)(2,1)}) custom-call(bf16[256,1792]{1,0:T(8,128)(2,1)} %copy-done.2, bf16[256,1792]{1,0:T(8,128)(2,1)} %copy-done.13, bf16[8,2,32,1792]{3,2,1,0:T(8,128)(2,1)} %get-tuple-element.158.refs_2_, ...), custom_call_target="tpu_custom_call" | custom-call | flops 3758096384 | bytes 14680064 | tf_op jit(solution)/shard_map/input_grad_terms/pallas_call | solution.py:201
  127.1 6.7 %collective-permute-done.24.refs_1_ = bf16[256,1792]{1,0:T(8,128)(2,1)S(1)} collective-permute-done((bf16[256,1792]{1,0:T(8,128)(2,1)S(1)}, bf16[256,1792]{1,0:T(8,128)(2,1)S(1)}, u32[]{:S(2)}, u32[]{:S(2)}) %collective-permute-start.24) | collective-permute-done | bytes 917536 | tf_op jit(solution)/shard_map/ppermute | solution.py:336
  133.8 0.9 copy-done.15
  134.7 12.9 %input_grad_terms.3 = (bf16[8,2,32,1792]{3,2,1,0:T(8,128)(2,1)}, bf16[8,2,32,1792]{3,2,1,0:T(8,128)(2,1)}, bf16[4,32,2048]{2,1,0:T(8,128)(2,1)}, bf16[4,32,2048]{2,1,0:T(8,128)(2,1)}) custom-call(bf16[256,1792]{1,0:T(8,128)(2,1)} %copy-done.3, bf16[256,1792]{1,0:T(8,128)(2,1)} %copy-done.15, ...), custom_call_target="tpu_custom_call", output_to_operand_aliasing={{0}: (6, {}), {1}: (7, {})} | custom-call | flops 3758096384 | bytes 14680064 | tf_op jit(solution)/shard_map/input_grad_terms/pallas_call | solution.py:201
  148.0 2.0 %collective-permute-done.26 = bf16[4,32,2048]{2,1,0:T(8,128)(2,1)S(1)} collective-permute-done((bf16[4,32,2048]{2,1,0:T(8,128)(2,1)}, bf16[4,32,2048]{2,1,0:T(8,128)(2,1)S(1)}, u32[]{:S(2)}, u32[]{:S(2)}) %collective-permute-start.26) | collective-permute-done | bytes 524320 | tf_op jit(solution)/shard_map/ppermute | solution.py:341
  150.2 1.6 collective-permute-start.27
  152.6 1.3 collective-permute-start.29
  154.0 13.4 %projection_grads.1 = (f32[2048,1792]{1,0:T(8,128)}, f32[2048,1792]{1,0:T(8,128)}) custom-call(bf16[2048,512]{1,0:T(8,128)(2,1)} %turned.1.inputs_ref, bf16[512,1792]{1,0:T(8,128)(2,1)} %bitcast.31, bf16[512,1792]{1,0:T(8,128)(2,1)} %bitcast.32), custom_call_target="tpu_custom_call" | custom-call | flops 7516192768 | bytes 29360128 | tf_op jit(solution)/shard_map/projection_grads/pallas_call | solution.py:234
  (97 shorter events, 12.3 us)
Async XLA Ops:
  0.6 20.9 %collective-permute-start.4 = (bf16[2,2,32,1792]{3,2,1,0:T(8,128)(2,1)}, bf16[2,2,32,1792]{3,2,1,0:T(8,128)(2,1)S(1)}, u32[]{:S(2)}, u32[]{:S(2)}) collective-permute-start(bf16[2,2,32,1792]{3,2,1,0:T(8,128)(2,1)} %bitcast.46), channel_id=1, source_target_pairs={{8,16},{16,8},{9,17},{17,9},{10,18},{18,10},{11,19},{19,11},{12,20... | collective-permute-start | bytes 1376264 | tf_op jit(solution)/shard_map/ppermute | solution.py:306
  1.3 20.2 %collective-permute-start.3 = (bf16[2,2,32,1792]{3,2,1,0:T(8,128)(2,1)}, bf16[2,2,32,1792]{3,2,1,0:T(8,128)(2,1)S(1)}, u32[]{:S(2)}, u32[]{:S(2)}) collective-permute-start(bf16[2,2,32,1792]{3,2,1,0:T(8,128)(2,1)} %bitcast.47), channel_id=1, source_target_pairs={{0,8},{8,0},{16,24},{24,16},{1,9},{9,1},{17,25},{25,17},{2,10},{10... | collective-permute-start | bytes 1376264 | tf_op jit(solution)/shard_map/ppermute | solution.py:306
  7.2 10.4 %collective-permute-start.2 = (bf16[2,32,2048]{2,1,0:T(8,128)(2,1)}, bf16[2,32,2048]{2,1,0:T(8,128)(2,1)S(1)}, u32[]{:S(2)}, u32[]{:S(2)}) collective-permute-start(bf16[2,32,2048]{2,1,0:T(8,128)(2,1)} %bitcast.33), channel_id=1, source_target_pairs={{0,6},{1,7},{2,4},{3,5},{4,2},{5,3},{6,0},{7,1},{8,14},{9,15},{10,... | collective-permute-start | bytes 786440 | tf_op jit(solution)/shard_map/ppermute | solution.py:275
  9.7 11.8 %collective-permute-start.1 = (bf16[2,32,2048]{2,1,0:T(8,128)(2,1)}, bf16[2,32,2048]{2,1,0:T(8,128)(2,1)S(1)}, u32[]{:S(2)}, u32[]{:S(2)}) collective-permute-start(bf16[2,32,2048]{2,1,0:T(8,128)(2,1)} %bitcast.34), channel_id=1, source_target_pairs={{0,4},{1,5},{2,6},{3,7},{4,0},{5,1},{6,2},{7,3},{8,12},{9,13},{10,... | collective-permute-start | bytes 786440 | tf_op jit(solution)/shard_map/ppermute | solution.py:275
  10.2 11.4 %collective-permute-start = (bf16[2,32,2048]{2,1,0:T(8,128)(2,1)}, bf16[2,32,2048]{2,1,0:T(8,128)(2,1)S(1)}, u32[]{:S(2)}, u32[]{:S(2)}) collective-permute-start(bf16[2,32,2048]{2,1,0:T(8,128)(2,1)} %bitcast.35), channel_id=1, source_target_pairs={{0,2},{1,3},{2,0},{3,1},{4,6},{5,7},{6,4},{7,5},{8,10},{9,11},{10,... | collective-permute-start | bytes 786440 | tf_op jit(solution)/shard_map/ppermute | solution.py:275
  21.6 3.4 %collective-permute-start.5 = (bf16[2,32,2048]{2,1,0:T(8,128)(2,1)}, bf16[2,32,2048]{2,1,0:T(8,128)(2,1)S(1)}, u32[]{:S(2)}, u32[]{:S(2)}) collective-permute-start(bf16[2,32,2048]{2,1,0:T(8,128)(2,1)} %bitcast.36), channel_id=1, source_target_pairs={{0,1},{1,0},{2,3},{3,2},{4,5},{5,4},{6,7},{7,6},{8,9},{9,8},{10,11... | collective-permute-start | bytes 786440 | tf_op jit(solution)/shard_map/ppermute | solution.py:280
  21.6 12.0 %collective-permute-start.10 = (bf16[2,2,32,1792]{3,2,1,0:T(8,128)(2,1)}, bf16[2,2,32,1792]{3,2,1,0:T(8,128)(2,1)S(1)}, u32[]{:S(2)}, u32[]{:S(2)}) collective-permute-start(bf16[2,2,32,1792]{3,2,1,0:T(8,128)(2,1)} %bitcast.43), channel_id=1, source_target_pairs={{8,16},{16,8},{9,17},{17,9},{10,18},{18,10},{11,19},{19,11},{12,20... | collective-permute-start | bytes 1376264 | tf_op jit(solution)/shard_map/ppermute | solution.py:306
  22.3 13.3 %collective-permute-start.9 = (bf16[2,2,32,1792]{3,2,1,0:T(8,128)(2,1)}, bf16[2,2,32,1792]{3,2,1,0:T(8,128)(2,1)}, u32[]{:S(2)}, u32[]{:S(2)}) collective-permute-start(bf16[2,2,32,1792]{3,2,1,0:T(8,128)(2,1)} %bitcast.44), channel_id=1, source_target_pairs={{0,8},{8,0},{16,24},{24,16},{1,9},{9,1},{17,25},{25,17},{2,10},{10... | collective-permute-start | bytes 1376264 | tf_op jit(solution)/shard_map/ppermute | solution.py:306
  24.4 1.5 collective-permute-start.6
  24.4 1.9 %collective-permute-start.7 = (bf16[2,32,2048]{2,1,0:T(8,128)(2,1)S(1)}, bf16[2,32,2048]{2,1,0:T(8,128)(2,1)S(1)}, u32[]{:S(2)}, u32[]{:S(2)}) collective-permute-start(bf16[2,32,2048]{2,1,0:T(8,128)(2,1)S(1)} %collective-permute-done.1.refs_2_), channel_id=1, source_target_pairs={{0,1},{1,0},{2,3},{3,2},{4,5},{5,4},{6,7},{7,6},{8,9},{9,8},{10,11... | collective-permute-start | bytes 786440 | tf_op jit(solution)/shard_map/ppermute | solution.py:280
  24.9 1.8 %collective-permute-start.8 = (bf16[2,32,2048]{2,1,0:T(8,128)(2,1)S(1)}, bf16[2,32,2048]{2,1,0:T(8,128)(2,1)S(1)}, u32[]{:S(2)}, u32[]{:S(2)}) collective-permute-start(bf16[2,32,2048]{2,1,0:T(8,128)(2,1)S(1)} %collective-permute-done.2.refs_3_), channel_id=1, source_target_pairs={{0,1},{1,0},{2,3},{3,2},{4,5},{5,4},{6,7},{7,6},{8,9},{9,8},{10,11... | collective-permute-start | bytes 786440 | tf_op jit(solution)/shard_map/ppermute | solution.py:280
  35.9 22.3 %collective-permute-start.11 = (bf16[256,1792]{1,0:T(8,128)(2,1)S(1)}, bf16[256,1792]{1,0:T(8,128)(2,1)}, u32[]{:S(2)}, u32[]{:S(2)}) collective-permute-start(bf16[256,1792]{1,0:T(8,128)(2,1)S(1)} %bitcast_select_fusion.1), channel_id=1, source_target_pairs={{0,8},{8,0},{16,24},{24,16},{1,9},{9,1},{17,25},{25,17},{2,10},{10... | collective-permute-start | bytes 2752520 | tf_op jit(solution)/shard_map/ppermute | solution.py:313
  39.1 20.6 %collective-permute-start.12 = (bf16[2,2,2,32,1792]{4,3,2,1,0:T(8,128)(2,1)S(1)}, bf16[2,2,2,32,1792]{4,3,2,1,0:T(8,128)(2,1)S(1)}, u32[]{:S(2)}, u32[]{:S(2)}) collective-permute-start(bf16[2,2,2,32,1792]{4,3,2,1,0:T(8,128)(2,1)S(1)} %pad_maximum_fusion.1), channel_id=1, source_target_pairs={{8,16},{16,8},{9,17},{17,9},{10,18},{18,10},{11,19},{19,11},{12,20... | collective-permute-start | bytes 2752520 | tf_op jit(solution)/shard_map/ppermute | solution.py:392
  59.7 23.0 %copy-start.11 = (bf16[2,2,2,32,1792]{4,3,2,1,0:T(8,128)(2,1)}, bf16[2,2,2,32,1792]{4,3,2,1,0:T(8,128)(2,1)S(1)}, u32[]{:S(2)}) copy-start(bf16[2,2,2,32,1792]{4,3,2,1,0:T(8,128)(2,1)S(1)} %collective-permute-done.12.refs_6_) | copy-start | bytes 2752516
  59.9 22.6 %collective-permute-start.14 = (bf16[256,1792]{1,0:T(8,128)(2,1)S(1)}, bf16[256,1792]{1,0:T(8,128)(2,1)S(1)}, u32[]{:S(2)}, u32[]{:S(2)}) collective-permute-start(bf16[256,1792]{1,0:T(8,128)(2,1)S(1)} %bitcast_select_fusion), channel_id=1, source_target_pairs={{0,8},{8,0},{16,24},{24,16},{1,9},{9,1},{17,25},{25,17},{2,10},{10... | collective-permute-start | bytes 2752520 | tf_op jit(solution)/shard_map/ppermute | solution.py:313
  63.3 19.5 %collective-permute-start.13 = (bf16[256,1792]{1,0:T(8,128)(2,1)S(1)}, bf16[256,1792]{1,0:T(8,128)(2,1)S(1)}, u32[]{:S(2)}, u32[]{:S(2)}) collective-permute-start(bf16[256,1792]{1,0:T(8,128)(2,1)S(1)} %add_convert_fusion.3), channel_id=1, source_target_pairs={{8,16},{16,8},{9,17},{17,9},{10,18},{18,10},{11,19},{19,11},{12,20... | collective-permute-start | bytes 2752520 | tf_op jit(solution)/shard_map/ppermute | solution.py:330
  64.0 19.5 %collective-permute-start.17 = (bf16[64,2048]{1,0:T(8,128)(2,1)S(1)}, bf16[64,2048]{1,0:T(8,128)(2,1)}, u32[]{:S(2)}, u32[]{:S(2)}) collective-permute-start(bf16[64,2048]{1,0:T(8,128)(2,1)S(1)} %copy-done.21), channel_id=1, source_target_pairs={{0,6},{1,7},{2,4},{3,5},{4,2},{5,3},{6,0},{7,1},{8,14},{9,15},{10,... | collective-permute-start | bytes 786440 | tf_op jit(solution)/shard_map/ppermute | solution.py:275
  65.7 17.8 %collective-permute-start.16 = (bf16[64,2048]{1,0:T(8,128)(2,1)S(1)}, bf16[64,2048]{1,0:T(8,128)(2,1)}, u32[]{:S(2)}, u32[]{:S(2)}) collective-permute-start(bf16[64,2048]{1,0:T(8,128)(2,1)S(1)} %copy-done.21), channel_id=1, source_target_pairs={{0,4},{1,5},{2,6},{3,7},{4,0},{5,1},{6,2},{7,3},{8,12},{9,13},{10,... | collective-permute-start | bytes 786440 | tf_op jit(solution)/shard_map/ppermute | solution.py:275
  67.0 16.5 %collective-permute-start.15 = (bf16[64,2048]{1,0:T(8,128)(2,1)S(1)}, bf16[64,2048]{1,0:T(8,128)(2,1)}, u32[]{:S(2)}, u32[]{:S(2)}) collective-permute-start(bf16[64,2048]{1,0:T(8,128)(2,1)S(1)} %copy-done.21), channel_id=1, source_target_pairs={{0,2},{1,3},{2,0},{3,1},{4,6},{5,7},{6,4},{7,5},{8,10},{9,11},{10,... | collective-permute-start | bytes 786440 | tf_op jit(solution)/shard_map/ppermute | solution.py:275
  83.5 16.2 %copy-start.2 = (bf16[256,1792]{1,0:T(8,128)(2,1)}, bf16[256,1792]{1,0:T(8,128)(2,1)S(1)}, u32[]{:S(2)}) copy-start(bf16[256,1792]{1,0:T(8,128)(2,1)S(1)} %add_convert_fusion.2.refs_0_) | copy-start | bytes 2752516
  83.5 16.2 %collective-permute-start.19 = (bf16[256,1792]{1,0:T(8,128)(2,1)S(1)}, bf16[256,1792]{1,0:T(8,128)(2,1)S(1)}, u32[]{:S(2)}, u32[]{:S(2)}) collective-permute-start(bf16[256,1792]{1,0:T(8,128)(2,1)S(1)} %add_convert_fusion.1), channel_id=1, source_target_pairs={{8,16},{16,8},{9,17},{17,9},{10,18},{18,10},{11,19},{19,11},{12,20... | collective-permute-start | bytes 2752520 | tf_op jit(solution)/shard_map/ppermute | solution.py:330
  84.2 24.4 %collective-permute-start.18 = (bf16[256,1792]{1,0:T(8,128)(2,1)S(1)}, bf16[256,1792]{1,0:T(8,128)(2,1)S(1)}, u32[]{:S(2)}, u32[]{:S(2)}) collective-permute-start(bf16[256,1792]{1,0:T(8,128)(2,1)S(1)} %add_convert_fusion.2.refs_0_), channel_id=1, source_target_pairs={{8,0},{16,24},{9,1},{17,25},{10,2},{18,26},{11,3},{19,27},{12,4},{... | collective-permute-start | bytes 2752520 | tf_op jit(solution)/shard_map/ppermute | solution.py:336
  85.5 17.0 %collective-permute-start.20 = (bf16[64,2048]{1,0:T(8,128)(2,1)S(1)}, bf16[64,2048]{1,0:T(8,128)(2,1)}, u32[]{:S(2)}, u32[]{:S(2)}) collective-permute-start(bf16[64,2048]{1,0:T(8,128)(2,1)S(1)} %copy-done.21), channel_id=1, source_target_pairs={{0,1},{1,0},{2,3},{3,2},{4,5},{5,4},{6,7},{7,6},{8,9},{9,8},{10,11... | collective-permute-start | bytes 786440 | tf_op jit(solution)/shard_map/ppermute | solution.py:280
  85.6 16.9 %collective-permute-start.21 = (bf16[64,2048]{1,0:T(8,128)(2,1)}, bf16[64,2048]{1,0:T(8,128)(2,1)}, u32[]{:S(2)}, u32[]{:S(2)}) collective-permute-start(bf16[64,2048]{1,0:T(8,128)(2,1)} %collective-permute-done.15.refs_1_), channel_id=1, source_target_pairs={{0,1},{1,0},{2,3},{3,2},{4,5},{5,4},{6,7},{7,6},{8,9},{9,8},{10,11... | collective-permute-start | bytes 786440 | tf_op jit(solution)/shard_map/ppermute | solution.py:280
  86.1 16.4 %collective-permute-start.22 = (bf16[64,2048]{1,0:T(8,128)(2,1)}, bf16[64,2048]{1,0:T(8,128)(2,1)}, u32[]{:S(2)}, u32[]{:S(2)}) collective-permute-start(bf16[64,2048]{1,0:T(8,128)(2,1)} %collective-permute-done.16.refs_2_), channel_id=1, source_target_pairs={{0,1},{1,0},{2,3},{3,2},{4,5},{5,4},{6,7},{7,6},{8,9},{9,8},{10,11... | collective-permute-start | bytes 786440 | tf_op jit(solution)/shard_map/ppermute | solution.py:280
  100.7 1.9 %collective-permute-start.23 = (bf16[64,2048]{1,0:T(8,128)(2,1)}, bf16[64,2048]{1,0:T(8,128)(2,1)S(1)}, u32[]{:S(2)}, u32[]{:S(2)}) collective-permute-start(bf16[64,2048]{1,0:T(8,128)(2,1)} %collective-permute-done.17.refs_3_), channel_id=1, source_target_pairs={{0,1},{1,0},{2,3},{3,2},{4,5},{5,4},{6,7},{7,6},{8,9},{9,8},{10,11... | collective-permute-start | bytes 786440 | tf_op jit(solution)/shard_map/ppermute | solution.py:280
  108.6 25.2 %collective-permute-start.24 = (bf16[256,1792]{1,0:T(8,128)(2,1)S(1)}, bf16[256,1792]{1,0:T(8,128)(2,1)S(1)}, u32[]{:S(2)}, u32[]{:S(2)}) collective-permute-start(bf16[256,1792]{1,0:T(8,128)(2,1)S(1)} %add_convert_fusion.refs_0_), channel_id=1, source_target_pairs={{8,0},{16,24},{9,1},{17,25},{10,2},{18,26},{11,3},{19,27},{12,4},{... | collective-permute-start | bytes 2752520 | tf_op jit(solution)/shard_map/ppermute | solution.py:336
  133.8 13.9 %collective-permute-start.25 = (bf16[4,32,2048]{2,1,0:T(8,128)(2,1)}, bf16[4,32,2048]{2,1,0:T(8,128)(2,1)S(1)}, u32[]{:S(2)}, u32[]{:S(2)}) collective-permute-start(bf16[4,32,2048]{2,1,0:T(8,128)(2,1)} %get-tuple-element.169), channel_id=1, source_target_pairs={{0,1},{1,0},{2,3},{3,2},{4,5},{5,4},{6,7},{7,6},{8,9},{9,8},{10,11... | collective-permute-start | bytes 1572872 | tf_op jit(solution)/shard_map/ppermute | solution.py:341
  147.8 2.2 %collective-permute-start.26 = (bf16[4,32,2048]{2,1,0:T(8,128)(2,1)}, bf16[4,32,2048]{2,1,0:T(8,128)(2,1)S(1)}, u32[]{:S(2)}, u32[]{:S(2)}) collective-permute-start(bf16[4,32,2048]{2,1,0:T(8,128)(2,1)} %get-tuple-element.180), channel_id=1, source_target_pairs={{0,1},{1,0},{2,3},{3,2},{4,5},{5,4},{6,7},{7,6},{8,9},{9,8},{10,11... | collective-permute-start | bytes 1572872 | tf_op jit(solution)/shard_map/ppermute | solution.py:341
  150.2 17.1 %collective-permute-start.27 = (bf16[64,2048]{1,0:T(8,128)(2,1)S(1)}, bf16[64,2048]{1,0:T(8,128)(2,1)S(1)}, u32[]{:S(2)}, u32[]{:S(2)}) collective-permute-start(bf16[64,2048]{1,0:T(8,128)(2,1)S(1)} %pad_maximum_fusion.2), channel_id=1, source_target_pairs={{0,2},{1,3},{2,0},{3,1},{4,6},{5,7},{6,4},{7,5},{8,10},{9,11},{10,... | collective-permute-start | bytes 786440 | tf_op jit(solution)/shard_map/ppermute | solution.py:355
  151.8 15.6 %collective-permute-start.28 = (bf16[64,2048]{1,0:T(8,128)(2,1)S(1)}, bf16[64,2048]{1,0:T(8,128)(2,1)S(1)}, u32[]{:S(2)}, u32[]{:S(2)}) collective-permute-start(bf16[64,2048]{1,0:T(8,128)(2,1)S(1)} %pad_maximum_fusion.3), channel_id=1, source_target_pairs={{0,4},{1,5},{2,6},{3,7},{4,0},{5,1},{6,2},{7,3},{8,12},{9,13},{10,... | collective-permute-start | bytes 786440 | tf_op jit(solution)/shard_map/ppermute | solution.py:355
  152.6 14.8 %collective-permute-start.29 = (bf16[64,2048]{1,0:T(8,128)(2,1)S(1)}, bf16[64,2048]{1,0:T(8,128)(2,1)S(1)}, u32[]{:S(2)}, u32[]{:S(2)}) collective-permute-start(bf16[64,2048]{1,0:T(8,128)(2,1)S(1)} %pad_maximum_fusion.4), channel_id=1, source_target_pairs={{0,6},{1,7},{2,4},{3,5},{4,2},{5,3},{6,0},{7,1},{8,14},{9,15},{10,... | collective-permute-start | bytes 786440 | tf_op jit(solution)/shard_map/ppermute | solution.py:355
  (21 other events, 117.3 us)
